TPU v7x, 128 devices: a whole 4x4x4 slice. The times are simulated.
128 devices in a mesh: gx: 16 (over x, y), gy: 8 (over z, core).
Axes of the slice: x: 4, y: 4, z: 4, core: 2. Of those that a mesh axis runs over, the one named last changes fastest.
Arguments:
- enthalpy_start: float32 [8, 128, 1024], P(None, 'gx', 'gy'), may hold values from -4 to 4
- tangent_start: float32 [16, 8, 128, 1024], P(None, None, 'gx', 'gy'), may hold values from -3 to 3
- labels: int32 [8, 128, 1024], P(None, 'gx', 'gy'), may hold values 0 or 1
- curve_parameters: float32 [16], replicated, may hold values from -0.1 to 0.1
- pixel_cells: int32 [131072], P(('gx', 'gy')), may hold values from 0 to 1023, as said below
- row_slot: int32 [131072], P(('gx', 'gy')), may hold values from 0 to 131071, as said below
Outputs:
- heat_content: float32 [8, 128, 1024], P(None, 'gx', 'gy')
- tangent_end: float32 [16, 8, 128, 1024], P(None, None, 'gx', 'gy')
- jacobian: float32 [16, 131072], P(None, ('gx', 'gy'))
Inputs may be any that keep to these rules, and one draw needn't show every extreme that they name: `pixel_cells`: the 1024 entries of each device's block are distinct cells of its own tile, numbered x * 128 + y within the tile. `row_slot`: A permutation of the rows; row r is owned by device r // 1024. Of one device's 1024 pixels at most 32 have rows of one owner, and every device has exactly 32 for some owner.
All inputs are finite; a program needn't handle non-finite values. No bound on the sum of `labels` on one device may be relied on, other than what follows from the above.
Results may differ from a plain program's by a relative error of at most 0.0001.
Values sent between devices are 32-bit elements; how exact they have to be, the bound alone decides.
A program may use at most 192 MiB of HBM per device.

v0:
```python
import jax
import jax.numpy as jnp
from jax import lax
from jax.sharding import PartitionSpec as P

STEPS = 8


step_rate = 0.15
knot_width = 0.3


def padded_2(shard, sides, width):
    for axis, dim in sides:
        peers, length = (lax.axis_size(axis), shard.shape[dim])
        up = [(i, (i + 1) % peers) for i in range(peers - 1)]
        down = [(j, i) for i, j in up]
        last = lax.slice_in_dim(shard, length - width, length, axis=dim)
        leading = lax.slice_in_dim(shard, 0, width, axis=dim)
        before = lax.ppermute(last, axis, up)
        after = lax.ppermute(leading, axis, down)
        shard = jnp.concatenate([before, shard, after], axis=dim)
    return shard


def conduction_advance(heat_content, direction_seed, melted_share, curve_parameters):
    parameter_total = curve_parameters.shape[0]
    knot_pos = -2.0 + 0.25 * (jnp.arange(parameter_total, dtype=jnp.float32) + 0.5)
    scaled = (heat_content[None] - knot_pos[:, None, None, None]) / knot_width
    kernel_shapes = jnp.exp(-scaled * scaled)
    bump_slope = -2.0 * scaled / knot_width * kernel_shapes
    scaled_kernels = curve_parameters[:, None, None, None]
    heat_level_grid = jnp.where(
        melted_share > 0,
        heat_content + jnp.sum(scaled_kernels * kernel_shapes, 0),
        0.5 * heat_content,
    )
    gradient_rate = jnp.where(melted_share > 0, 1.0 + jnp.sum(scaled_kernels * bump_slope, 0), 0.5)
    heat_level_derivative = (
        gradient_rate[None] * direction_seed + melted_share[None] * kernel_shapes
    )
    return (heat_level_grid, heat_level_derivative)


def neighbours(padded):
    return [
        padded[..., 2:, 1:-1, 1:-1],
        padded[..., :-2, 1:-1, 1:-1],
        padded[..., 1:-1, 2:, 1:-1],
        padded[..., 1:-1, :-2, 1:-1],
        padded[..., 1:-1, 1:-1, 2:],
        padded[..., 1:-1, 1:-1, :-2],
    ]


def face_weights(conduct, padded):
    return [2.0 * conduct * other / (conduct + other) for other in neighbours(padded)]


def spread(padded, sensitivity_matrix, weights):
    net_flow = jnp.zeros_like(sensitivity_matrix)
    for weight, other in zip(weights, neighbours(padded)):
        net_flow = net_flow + weight[None] * (other - sensitivity_matrix)
    return net_flow


def local(enthalpy_start, tangent_start, labels, curve_parameters, pixel_cells, row_slot):
    melted_share = (labels == 1).astype(jnp.float32)
    conduct = jnp.where(labels == 1, 0.5, 1.0).astype(jnp.float32)
    conduct_rim = padded_2(conduct, (("gx", 1), ("gy", 2)), 1)
    conduct_rim = jnp.pad(conduct_rim, ((1, 1), (0, 0), (0, 0)))
    weights = face_weights(conduct, conduct_rim)
    heat_content, direction_seed = (enthalpy_start, tangent_start)
    for repeat in range(STEPS):
        heat_level_grid, heat_level_derivative = conduction_advance(
            heat_content, direction_seed, melted_share, curve_parameters
        )
        sensitivity_matrix = jnp.concatenate([heat_level_grid[None], heat_level_derivative], 0)
        padded = padded_2(sensitivity_matrix, (("gx", 2), ("gy", 3)), 1)
        padded = jnp.pad(padded, ((0, 0), (1, 1), (0, 0), (0, 0)))
        net_flow = spread(padded, sensitivity_matrix, weights)
        heat_content = heat_content + step_rate * net_flow[0]
        direction_seed = direction_seed + step_rate * net_flow[1:]
    heat_level_grid, heat_level_derivative = conduction_advance(
        heat_content, direction_seed, melted_share, curve_parameters
    )
    parameter_total = curve_parameters.shape[0]
    boundary_layer = heat_level_derivative[:, -1].reshape(parameter_total, -1)
    pixel_rows = jnp.take(boundary_layer, pixel_cells, axis=1)
    pixel_count = pixel_cells.shape[0]
    size_x = lax.axis_size("gx")
    size_y = lax.axis_size("gy")
    devices = size_x * size_y
    dense_block = (
        jnp.zeros((parameter_total, devices * pixel_count), jnp.float32)
        .at[:, row_slot]
        .set(pixel_rows)
    )
    jacobian = lax.psum_scatter(dense_block, ("gx", "gy"), scatter_dimension=1, tiled=True)
    return (heat_content, direction_seed, jacobian)


def solution(mesh):
    in_specs = (
        P(None, "gx", "gy"),
        P(None, None, "gx", "gy"),
        P(None, "gx", "gy"),
        P(),
        P(("gx", "gy")),
        P(("gx", "gy")),
    )
    out_specs = (P(None, "gx", "gy"), P(None, None, "gx", "gy"), P(None, ("gx", "gy")))
    return jax.shard_map(local, mesh=mesh, in_specs=in_specs, out_specs=out_specs, check_vma=False)
```

profile of v0, /device:TPU:1, one launch (start us, length us, event | category | flops | bytes accessed | tf_op | source)
XLA Modules:
  0.0 1052.4 jit_solution(5156451940894531941)
XLA Ops:
  8.0 4.0 collective-permute-start
  12.0 1.3 collective-permute-start.1
  13.3 3.0 collective-permute-done.1
  16.5 4.0 collective-permute-start.3
  20.5 3.4 collective-permute-start.2
  27.7 3.2 collective-permute-start.4
  30.9 1.3 collective-permute-start.5
  32.3 4.0 collective-permute-done.5
  37.5 2.2 collective-permute-start.7
  40.3 5.2 collective-permute-start.6
  48.1 2.5 select_maximum_fusion.35
  50.7 2.4 fusion.111
  53.8 4.2 collective-permute-start.8
  58.0 1.3 collective-permute-start.9
  59.3 4.0 collective-permute-done.9
  65.8 1.9 collective-permute-start.11
  68.4 5.6 collective-permute-start.10
  75.3 2.1 copy.144
  77.4 3.4 select_maximum_fusion.30
  83.5 3.7 collective-permute-start.12
  88.6 4.0 collective-permute-done.13
  93.9 1.9 collective-permute-start.15
  96.5 4.9 collective-permute-start.14
  103.9 2.5 select_maximum_fusion.25
  106.5 2.3 fusion.81
  109.5 3.7 collective-permute-start.16
  113.2 1.5 collective-permute-start.17
  114.7 3.8 collective-permute-done.17
  121.0 1.9 collective-permute-start.19
  123.6 5.2 collective-permute-start.18
  130.1 2.1 copy.156
  132.2 3.4 select_maximum_fusion.20
  138.3 3.8 collective-permute-start.20
  142.1 1.3 collective-permute-start.21
  143.4 4.0 collective-permute-done.21
  148.7 1.9 collective-permute-start.23
  151.3 5.5 collective-permute-start.22
  159.4 2.5 select_maximum_fusion.15
  161.9 2.3 fusion.51
  164.9 3.7 collective-permute-start.24
  170.0 4.0 collective-permute-done.25
  176.5 1.9 collective-permute-start.27
  179.1 4.9 collective-permute-start.26
  185.3 2.1 copy.168
  187.4 3.4 select_maximum_fusion.10
  193.6 3.7 collective-permute-start.28
  197.3 1.7 collective-permute-start.29
  199.1 3.6 collective-permute-done.29
  204.6 5.3 collective-permute-start.30
  209.9 1.9 collective-permute-start.31
  211.8 4.4 sort
  218.8 2.5 select_maximum_fusion.5
  221.4 2.3 fusion.21
  224.4 3.7 collective-permute-start.32
  230.0 3.4 collective-permute-done.33
  236.6 4.8 collective-permute-start.34
  241.4 2.1 collective-permute-start.35
  244.8 2.1 collective-permute-done.35
  248.3 2.1 copy.180
  250.3 3.4 select_maximum_fusion
  255.8 2.8 gather_fusion
  258.8 38.6 %scatter_custom_fusion = f32[16,131072]{0,1:T(8,128)} fusion(s32[1024]{0:T(1024)} %get-tuple-element.12, f32[]{:T(128)} %constant.72.clone.1, f32[1024,16]{1,0:T(8,128)S(1)} %broadcast_select_fusion, s32[1024]{0:T(1024)} %broadcast_clamp_fusion), kind=kCustom, calls=%fused_computation.3 | custom fusion | bytes 8389120 | tf_op jit(solution)/shard_map/scatter | solution.py:97
  297.5 746.0 %reduce-scatter.2.cloned.1.call-done = f32[16,1024]{0,1:T(8,128)} async-done(((f32[16,131072]{0,1:T(8,128)}), f32[16,1024]{0,1:T(8,128)}) %reduce-scatter.2.cloned.1.call-update) | async-done | bytes 65552 | tf_op jit(solution)/shard_map/reduce_scatter | solution.py:99
  1043.5 1.8 copy.185
  (289 shorter events, 59.2 us)
Async XLA Ops:
  7.2 1036.4 %reduce-scatter.2.cloned.1.call-start = ((), (), s32[]{:S(2)}) async-start(), calls=%async_computation.1 | async-start | bytes 67633152 | tf_op jit(solution)/shard_map/reduce_scatter | solution.py:99
  8.0 5.4 collective-permute-start
  12.0 4.4 collective-permute-start.1
  16.5 8.6 collective-permute-start.3
  20.5 4.8 collective-permute-start.2
  25.0 219.8 %copy-start.8 = (f32[8,8,128]{2,1,0:T(8,128)}, f32[8,8,128]{2,1,0:T(8,128)S(1)}, u32[]{:S(2)}) copy-start(f32[8,8,128]{2,1,0:T(8,128)S(1)} %convert_element_type.14) | copy-start | bytes 98308
  26.3 21.8 %copy-start.9 = (f32[1,8,8,128]{3,2,1,0:T(8,128)}, f32[1,8,8,128]{3,2,1,0:T(8,128)S(1)}, u32[]{:S(2)}) copy-start(f32[1,8,8,128]{3,2,1,0:T(8,128)S(1)} %get-tuple-element.84) | copy-start | bytes 98308
  27.7 4.6 collective-permute-start.4
  30.9 5.3 collective-permute-start.5
  32.3 15.8 %copy-start.34 = (f32[17,8,1,128]{3,2,1,0:T(1,128)}, f32[17,8,1,128]{3,2,1,0:T(1,128)S(1)}, u32[]{:S(2)}) copy-start(f32[17,8,1,128]{3,2,1,0:T(1,128)S(1)} %collective-permute-done.4) | copy-start | bytes 208900
  36.2 11.9 %copy-start.43 = (f32[17,8,1,128]{3,2,1,0:T(1,128)}, f32[17,8,1,128]{3,2,1,0:T(1,128)S(1)}, u32[]{:S(2)}) copy-start(f32[17,8,1,128]{3,2,1,0:T(1,128)S(1)} %collective-permute-done.5) | copy-start | bytes 208900
  37.5 8.0 collective-permute-start.7
  40.3 6.5 collective-permute-start.6
  53.4 9.9 copy-start.25
  53.8 5.5 collective-permute-start.8
  58.0 5.3 collective-permute-start.9
  65.8 8.2 collective-permute-start.11
  68.4 6.9 collective-permute-start.10
  82.0 10.6 %copy-start.56 = (f32[8,8,128]{2,1,0:T(8,128)}, f32[8,8,128]{2,1,0:T(8,128)S(1)}, u32[]{:S(2)}) copy-start(f32[8,8,128]{2,1,0:T(8,128)S(1)} %fusion.246) | copy-start | bytes 98308
  82.3 10.3 copy-start.18
  83.5 5.1 collective-permute-start.12
  87.3 5.3 collective-permute-start.13
  88.6 15.3 %copy-start.37 = (f32[17,8,1,128]{3,2,1,0:T(1,128)}, f32[17,8,1,128]{3,2,1,0:T(1,128)S(1)}, u32[]{:S(2)}) copy-start(f32[17,8,1,128]{3,2,1,0:T(1,128)S(1)} %collective-permute-done.12) | copy-start | bytes 208900
  92.6 11.3 %copy-start.46 = (f32[17,8,1,128]{3,2,1,0:T(1,128)}, f32[17,8,1,128]{3,2,1,0:T(1,128)S(1)}, u32[]{:S(2)}) copy-start(f32[17,8,1,128]{3,2,1,0:T(1,128)S(1)} %collective-permute-done.13) | copy-start | bytes 208900
  93.2 10.7 %copy-start.19 = (f32[1,8,8,128]{3,2,1,0:T(8,128)S(1)}, f32[1,8,8,128]{3,2,1,0:T(8,128)}, u32[]{:S(2)}) copy-start(f32[1,8,8,128]{3,2,1,0:T(8,128)} %copy-done.18) | copy-start | bytes 98308
  93.9 7.5 collective-permute-start.15
  96.5 6.2 collective-permute-start.14
  108.8 10.9 %copy-start.60 = (f32[8,8,128]{2,1,0:T(8,128)}, f32[8,8,128]{2,1,0:T(8,128)S(1)}, u32[]{:S(2)}) copy-start(f32[8,8,128]{2,1,0:T(8,128)S(1)} %fusion.244) | copy-start | bytes 98308
  109.5 5.2 collective-permute-start.16
  113.2 5.3 collective-permute-start.17
  121.0 7.8 collective-permute-start.19
  123.6 6.5 collective-permute-start.18
  136.8 10.6 %copy-start.54 = (f32[8,8,128]{2,1,0:T(8,128)}, f32[8,8,128]{2,1,0:T(8,128)S(1)}, u32[]{:S(2)}) copy-start(f32[8,8,128]{2,1,0:T(8,128)S(1)} %fusion.242) | copy-start | bytes 98308
  137.2 10.3 copy-start.15
  138.3 5.1 collective-permute-start.20
  142.1 5.3 collective-permute-start.21
  143.4 15.9 %copy-start.40 = (f32[17,8,1,128]{3,2,1,0:T(1,128)}, f32[17,8,1,128]{3,2,1,0:T(1,128)S(1)}, u32[]{:S(2)}) copy-start(f32[17,8,1,128]{3,2,1,0:T(1,128)S(1)} %collective-permute-done.20) | copy-start | bytes 208900
  147.4 11.9 %copy-start.49 = (f32[17,8,1,128]{3,2,1,0:T(1,128)}, f32[17,8,1,128]{3,2,1,0:T(1,128)S(1)}, u32[]{:S(2)}) copy-start(f32[17,8,1,128]{3,2,1,0:T(1,128)S(1)} %collective-permute-done.21) | copy-start | bytes 208900
  148.0 11.3 %copy-start.16 = (f32[1,8,8,128]{3,2,1,0:T(8,128)S(1)}, f32[1,8,8,128]{3,2,1,0:T(8,128)}, u32[]{:S(2)}) copy-start(f32[1,8,8,128]{3,2,1,0:T(8,128)} %copy-done.15) | copy-start | bytes 98308
  148.7 8.1 collective-permute-start.23
  151.3 6.8 collective-permute-start.22
  164.2 11.0 %copy-start.62 = (f32[8,8,128]{2,1,0:T(8,128)}, f32[8,8,128]{2,1,0:T(8,128)S(1)}, u32[]{:S(2)}) copy-start(f32[8,8,128]{2,1,0:T(8,128)S(1)} %fusion.240) | copy-start | bytes 98308
  164.5 9.5 copy-start.23
  164.9 5.1 collective-permute-start.24
  168.7 5.3 collective-permute-start.25
  176.5 7.5 collective-permute-start.27
  179.1 6.2 collective-permute-start.26
  192.1 10.6 %copy-start.52 = (f32[8,8,128]{2,1,0:T(8,128)}, f32[8,8,128]{2,1,0:T(8,128)S(1)}, u32[]{:S(2)}) copy-start(f32[8,8,128]{2,1,0:T(8,128)S(1)} %fusion.238) | copy-start | bytes 98308
  192.4 10.3 copy-start.10
  193.6 5.5 collective-permute-start.28
  197.3 5.3 collective-permute-start.29
  199.1 19.7 %copy-start.30 = (f32[17,8,1,128]{3,2,1,0:T(1,128)}, f32[17,8,1,128]{3,2,1,0:T(1,128)S(1)}, u32[]{:S(2)}) copy-start(f32[17,8,1,128]{3,2,1,0:T(1,128)S(1)} %collective-permute-done.28) | copy-start | bytes 208900
  202.7 16.1 %copy-start.33 = (f32[17,8,1,128]{3,2,1,0:T(1,128)}, f32[17,8,1,128]{3,2,1,0:T(1,128)S(1)}, u32[]{:S(2)}) copy-start(f32[17,8,1,128]{3,2,1,0:T(1,128)S(1)} %collective-permute-done.29) | copy-start | bytes 208900
  203.3 15.5 %copy-start.11 = (f32[1,8,8,128]{3,2,1,0:T(8,128)S(1)}, f32[1,8,8,128]{3,2,1,0:T(8,128)}, u32[]{:S(2)}) copy-start(f32[1,8,8,128]{3,2,1,0:T(8,128)} %copy-done.10) | copy-start | bytes 98308
  204.6 12.9 %collective-permute-start.30 = (f32[17,8,10,1]{0,1,3,2:T(8,128)S(1)}, f32[17,8,10,1]{0,1,3,2:T(8,128)S(1)}, u32[]{:S(2)}, u32[]{:S(2)}) collective-permute-start(f32[17,8,10,1]{0,1,3,2:T(8,128)S(1)} %copy.172), channel_id=1, source_target_pairs={{0,1},{1,2},{2,3},{3,4},{4,5},{5,6},{6,7},{8,9},{9,10},{10,11},{11... | collective-permute-start | bytes 16328 | tf_op jit(solution)/shard_map/ppermute | solution.py:20
  209.9 6.3 collective-permute-start.31
  223.7 11.0 %copy-start.58 = (f32[8,8,128]{2,1,0:T(8,128)}, f32[8,8,128]{2,1,0:T(8,128)S(1)}, u32[]{:S(2)}) copy-start(f32[8,8,128]{2,1,0:T(8,128)S(1)} %fusion.236) | copy-start | bytes 98308
  224.0 9.5 copy-start.13
  224.4 5.7 collective-permute-start.32
  228.1 5.3 collective-permute-start.33
  236.6 11.6 %collective-permute-start.34 = (f32[17,8,10,1]{0,1,3,2:T(8,128)S(1)}, f32[17,8,10,1]{0,1,3,2:T(8,128)}, u32[]{:S(2)}, u32[]{:S(2)}) collective-permute-start(f32[17,8,10,1]{0,1,3,2:T(8,128)S(1)} %copy.178), channel_id=1, source_target_pairs={{0,1},{1,2},{2,3},{3,4},{4,5},{5,6},{6,7},{8,9},{9,10},{10,11},{11... | collective-permute-start | bytes 16328 | tf_op jit(solution)/shard_map/ppermute | solution.py:20
  241.4 5.5 collective-permute-start.35
  255.0 42.4 %copy-start.67 = (f32[8,8,128]{2,1,0:T(8,128)}, f32[8,8,128]{2,1,0:T(8,128)S(1)}, u32[]{:S(2)}) copy-start(f32[8,8,128]{2,1,0:T(8,128)S(1)} %fusion.234) | copy-start | bytes 98308
  255.5 42.0 %copy-start.27 = (f32[16,8,8,128]{3,2,1,0:T(8,128)}, f32[16,8,8,128]{3,2,1,0:T(8,128)S(1)}, u32[]{:S(2)}) copy-start(f32[16,8,8,128]{3,2,1,0:T(8,128)S(1)} %get-tuple-element.100) | copy-start | bytes 1572868
  (49 other events, 142.5 us)
Sparse Core Ops, SparseCore 0:
  297.6 745.8 reduce-scatter.1
where the time goes:
time: 1070 us; the launch traced here: 1050 us
  waiting for transfers between devices  782 us (73%)
  starting transfers between devices  111 us (10%)
  local copies, waits for them, and re-layouts  86.2 us (8%)
  other arithmetic  57.1 us (5%)
  between operations  16 us (1%)
    reduce_scatter x1, waiting for transfers between devices, local(): lax.psum_scatter(dense_block, ('gx', 'gy'), scatter_dimension=1, tiled=True)  746 us
    ppermute x18, starting transfers between devices, padded_2(): before = lax.ppermute(last, axis, up)  78.7 us
    scatter x2, local copies, waits for them, and re-layouts, local(): dense_block = jnp.zeros((parameter_total, devices * pixel_count), jnp.flo...  38.6 us
    ppermute x18, waiting for transfers between devices, padded_2(): after = lax.ppermute(leading, axis, down)  35.9 us
    ppermute x18, starting transfers between devices, padded_2(): after = lax.ppermute(leading, axis, down)  31.9 us
    concatenate x18, other arithmetic, padded_2(): shard = jnp.concatenate([before, shard, after], axis=dim)  25.3 us
  transfers between devices with their start and end apart: 37, of which 12 were waited for; matrix products, arithmetic and copies ran while one was open for 2% of the time, Pallas kernels for 0%

commit v1 on v0

v1 whole, which is shorter than its diff:
```python
import functools
import math

import jax
import jax.numpy as jnp
from jax import lax
from jax.experimental import pallas as pl
from jax.experimental.pallas import tpu as pltpu
from jax.sharding import PartitionSpec as P

STEPS = 8
COEF = 16
RATE = 0.15
WIDTH = 0.3
ROOT = math.sqrt(math.log2(math.e))
KNOTS = [-2.0 + 0.25 * (j + 0.5) for j in range(COEF)]

MAIN = 24
STRIP = 12
ALL = MAIN + STRIP
MOST = 32
MESH = pl.DeviceIdType.MESH


def lanes():
    return lax.broadcasted_iota(jnp.int32, (8, 128), 1)


def turn(v, shift, axis):
    size = v.shape[axis]
    shift = shift % size
    return v if shift == 0 else pltpu.roll(v, shift, axis)


def pack_edges(rows):
    chunk = lanes() // 8
    last = first = None
    for par in range(2):
        for x in range(8):
            at = par * 64 + x * 8
            a = turn(rows[par][x], at - 120, 1)
            b = turn(rows[par][x], at, 1)
            if last is None:
                last, first = a, b
            else:
                here = chunk == par * 8 + x
                last = jnp.where(here, a, last)
                first = jnp.where(here, b, first)
    return last, first


def build_strips(main, before, after, par):
    lane = lanes()
    block, inside = lane // 32, lane % 32
    out = []
    for g in range(STRIP):
        lo, hi = g, g + 12
        v = turn(main[lo], 8, 1)
        v = jnp.where(block == 1, turn(main[hi], 40, 1), v)
        v = jnp.where(block == 2, turn(main[lo], 80, 1), v)
        v = jnp.where(block == 3, turn(main[hi], 112, 1), v)
        for b, i in ((0, lo), (1, hi)):
            start = par * 64 + (i % 8) * 8
            left = turn(before[i // 8], b * 32 - start, 1)
            v = jnp.where((block == b) & (inside < 8), left, v)
            right = turn(after[i // 8], 64 + b * 32 + 16 - start, 1)
            v = jnp.where((block == b + 2) & (inside >= 16), right, v)
        out.append(v)
    return out


def merge(main, strips):
    lane = lanes()
    out = []
    for x in range(8):
        i = x + 8
        b, g = (0, i) if i < 12 else (1, i - 12)
        v = jnp.where(lane < 8, turn(strips[g], -(b * 32 + 8), 1), main[i])
        v = jnp.where(lane >= 120, turn(strips[g], 120 - (64 + b * 32 + 8), 1), v)
        out.append(v)
    return out


def advance(step, state, temp, wx, wy, wz):
    new = list(state)

    def own(i, t):
        fy = wy(i) * (turn(t, -1, 1) - t)
        fz = wz(i) * (turn(t, -1, 0) - t)
        return (fy - turn(fy, 1, 1)) + (fz - turn(fz, 1, 0))

    lo, hi = step, MAIN - step
    t = temp(lo)
    t_next = temp(lo + 1)
    flux = wx(lo) * (t_next - t)
    for i in range(lo + 1, hi - 1):
        t, t_next = t_next, temp(i + 1)
        below, flux = flux, wx(i) * (t_next - t)
        new[i] = state[i] + ((flux - below) + own(i, t))
    first = temp(MAIN)
    end = temp(ALL - 1)
    last_flux = wx(ALL - 1) * (turn(first, -32, 1) - end)
    below = turn(last_flux, 32, 1)
    t_next = first
    for i in range(MAIN, ALL):
        t = t_next
        if i == ALL - 1:
            flux = last_flux
        else:
            t_next = temp(i + 1) if i + 1 < ALL - 1 else end
            flux = wx(i) * (t_next - t)
        new[i] = state[i] + ((flux - below) + own(i, t))
        below = flux
    return new


def steps_kernel(
    n_gx, n_gy,
    e_ref, t_ref, lab_ref, coef_ref,
    e_out, t_out, v_out,
    el, hx_e, hx_t, pk, hp, est, tst, wst, sl, bump,
    se_sem, re_sem, st_sem, rt_sem, sp_sem, rp_sem,
):
    gx, gy = lax.axis_index("gx"), lax.axis_index("gy")

    def at(dx, dy):
        return lax.rem(gx + dx + n_gx, n_gx), lax.rem(gy + dy + n_gy, n_gy)

    around = [(dx, dy) for dx in (-1, 0, 1) for dy in (-1, 0, 1) if (dx, dy) != (0, 0)]
    barrier = pltpu.get_barrier_semaphore()
    for dx, dy in around:
        pl.semaphore_signal(barrier, inc=1, device_id=at(dx, dy), device_id_type=MESH)

    el[0:64, :] = e_ref[...]
    el[64:128, :] = jnp.where(lab_ref[...] == 1, 1.0, 0.0)
    pl.semaphore_wait(barrier, len(around))

    def send_e(d):
        return pltpu.make_async_remote_copy(
            el, hx_e.at[d], se_sem.at[d], re_sem.at[d], device_id=at(1 - 2 * d, 0), device_id_type=MESH
        )

    def send_t(q, d):
        part = pl.ds(q * 128, 128)
        return pltpu.make_async_remote_copy(
            t_ref.at[part], hx_t.at[d, part], st_sem.at[q, d], rt_sem.at[q, d],
            device_id=at(1 - 2 * d, 0), device_id_type=MESH,
        )

    def send_p(part, dx, dy):
        rows = pl.ds(0, 8) if part == 0 else pl.ds(8, 64)
        side = 0 if dy == 1 else 1
        return pltpu.make_async_remote_copy(
            pk.at[side, rows], hp.at[1 - dx, side, rows],
            sp_sem.at[part, dx + 1, side], rp_sem.at[part, 1 - dx, side],
            device_id=at(dx, dy), device_id_type=MESH,
        )

    corners = [(dx, dy) for dx in (0, -1, 1) for dy in (-1, 1)]
    for d in range(2):
        send_e(d).start()
    rows = [[el[pl.ds(par * 64 + x, 8, stride=8), :] for x in range(8)] for par in range(2)]
    last, first = pack_edges(rows)
    pk[0, 0:8, :] = last
    pk[1, 0:8, :] = first
    for dx, dy in corners:
        send_p(0, dx, dy).start()
    for q in range(2):
        for d in range(2):
            send_t(q, d).start()

    def pack_pair(q, _):
        rows = [[t_ref[pl.ds(q * 128 + par * 64 + x, 8, stride=8), :] for x in range(8)] for par in range(2)]
        last, first = pack_edges(rows)
        to = pl.ds(pl.multiple_of(8 + q * 8, 8), 8)
        pk[0, to, :] = last
        pk[1, to, :] = first
        return 0

    lax.fori_loop(0, 8, pack_pair, 0)
    for dx, dy in corners:
        send_p(1, dx, dy).start()

    def send_more(q, _):
        for d in range(2):
            send_t(q, d).start()
        return 0

    lax.fori_loop(2, 8, send_more, 0)

    for d in range(2):
        send_e(d).wait()
    for dx, dy in corners:
        send_p(0, dx, dy).wait()

    def rows_of(own, halo, base):
        got = [halo[0, pl.ds(base + x, 8, stride=8), :] for x in range(8)]
        got += [own[pl.ds(base + x, 8, stride=8), :] for x in range(8)]
        got += [halo[1, pl.ds(base + x, 8, stride=8), :] for x in range(8)]
        return got

    def strips_of(main, q, par):
        part = pl.ds(pl.multiple_of(q * 8, 8), 8)
        before = [hp[k, 0, part, :] for k in range(3)]
        after = [hp[k, 1, part, :] for k in range(3)]
        return build_strips(main, before, after, par)

    main = rows_of(el, hx_e, 64)
    pcm = main + strips_of(main, 0, 1)
    main = rows_of(el, hx_e, 0)
    start = main + strips_of(main, 0, 0)
    for i in range(ALL):
        est[i] = start[i]
        est[ALL + i] = pcm[i]

    lane = lanes()
    block, inside = lane // 32, lane % 32
    layer = lax.broadcasted_iota(jnp.int32, (8, 128), 0)
    open_x0 = jnp.where(gx == 0, 0.0, 1.0)
    open_x1 = jnp.where(gx == n_gx - 1, 0.0, 1.0)
    open_y0 = jnp.where(gy == 0, 0.0, 1.0)
    open_y1 = jnp.where(gy == n_gy - 1, 0.0, 1.0)
    cond = [1.0 - 0.5 * p for p in pcm]

    def face(a, b):
        return (2.0 * RATE) * a * b / (a + b)

    edge_y = jnp.where((block < 2) & (inside == 7), open_y0, 1.0)
    edge_y = jnp.where((block >= 2) & (inside == 15), open_y1, edge_y)
    for i in range(ALL):
        c = cond[i]
        if i == MAIN - 1:
            up = c
        elif i == ALL - 1:
            up = turn(cond[MAIN], -32, 1)
        else:
            up = cond[i + 1]
        wx = face(c, up)
        if i == 7:
            wx = wx * open_x0
        if i == 15:
            wx = wx * open_x1
        if i == MAIN + 7:
            wx = wx * jnp.where(block % 2 == 0, open_x0, 1.0)
        if i == MAIN + 3:
            wx = wx * jnp.where(block % 2 == 1, open_x1, 1.0)
        wst[i] = wx
        wy = face(c, turn(c, -1, 1))
        wst[ALL + i] = wy * edge_y if i >= MAIN else wy
        wst[2 * ALL + i] = jnp.where(layer == 7, 0.0, face(c, turn(c, -1, 0)))

    def shape_row(s, i):
        e = est[i]
        p = est[ALL + i] > 0
        scaled = jnp.where(p, e, 100.0) * (ROOT / WIDTH)
        total = jnp.zeros((8, 128), jnp.float32)
        slope = jnp.zeros((8, 128), jnp.float32)
        for j in range(COEF):
            v = scaled - KNOTS[j] * (ROOT / WIDTH)
            b = jnp.exp2(-(v * v))
            bump[(s * COEF + j) * ALL + i] = b
            cb = coef_ref[j] * b
            total = total + cb
            slope = slope + v * cb
        half = jnp.where(p, 1.0, 0.5)
        tst[i] = half * e + total
        sl[s * ALL + i] = half - (2.0 / (WIDTH * ROOT)) * slope

    for s in range(STEPS):
        def one(i, _, s=s):
            shape_row(s, i)
            return 0

        lax.fori_loop(s, MAIN - s, one, 0)
        lax.fori_loop(MAIN, ALL, one, 0)
        state = [est[i] for i in range(ALL)]
        new = advance(
            s, state, lambda i: tst[i], lambda i: wst[i], lambda i: wst[ALL + i], lambda i: wst[2 * ALL + i]
        )
        for i in range(ALL):
            if new[i] is not state[i]:
                est[i] = new[i]

    done = merge([est[i] for i in range(MAIN)], [est[MAIN + g] for g in range(STRIP)])
    for x in range(8):
        e_out[pl.ds(x, 8, stride=8), :] = done[x]

    for dx, dy in corners:
        send_p(1, dx, dy).wait()

    e7 = e_out[56:64, :]
    p7 = el[120:128, :] > 0
    scaled7 = jnp.where(p7, e7, 100.0) * (ROOT / WIDTH)
    slope7 = jnp.zeros((8, 128), jnp.float32)
    for j in range(COEF):
        v = scaled7 - KNOTS[j] * (ROOT / WIDTH)
        b = jnp.exp2(-(v * v))
        v_out[j * 8 : j * 8 + 8, :] = b
        slope7 = slope7 + v * (coef_ref[j] * b)
    slope7 = jnp.where(p7, 1.0, 0.5) - (2.0 / (WIDTH * ROOT)) * slope7

    def pair(q, _):
        for d in range(2):
            send_t(q, d).wait()
        for par in range(2):
            j = q * 2 + par
            main = rows_of(t_ref, hx_t, q * 128 + par * 64)
            state = main + strips_of(main, q + 1, par)
            for s in range(STEPS):
                def temp(i, s=s, state=state):
                    return sl[s * ALL + i] * state[i] + bump[(s * COEF + j) * ALL + i]

                state = advance(
                    s, state, temp, lambda i: wst[i], lambda i: wst[ALL + i], lambda i: wst[2 * ALL + i]
                )
            done = merge(state[:MAIN], state[MAIN:])
            for x in range(8):
                t_out[pl.ds(q * 128 + par * 64 + x, 8, stride=8), :] = done[x]
            at7 = pl.ds(pl.multiple_of(q * 128 + par * 64 + 56, 8), 8)
            to = pl.ds(pl.multiple_of(q * 16 + par * 8, 8), 8)
            v_out[to, :] = slope7 * t_out[at7, :] + v_out[to, :]
        return 0

    lax.fori_loop(0, 8, pair, 0)


def nt(a, b):
    return lax.dot_general(a, b, (((1,), (1,)), ((), ())), preferred_element_type=jnp.float32)


def rows_kernel(
    n_gx, n_gy,
    v_ref, cell_ref, slot_ref, out_ref,
    a_ref, m_ref, snd, rcv, lhs, rhs, local_sem, send_sem, recv_sem,
):
    n = n_gx * n_gy
    gx, gy = lax.axis_index("gx"), lax.axis_index("gy")
    me = gx * n_gy + gy
    barrier = pltpu.get_barrier_semaphore()

    def other(i):
        t = lax.rem(me + i, n)
        return t, (t // n_gy, lax.rem(t, n_gy))

    def greet(i, _):
        pl.semaphore_signal(barrier, inc=1, device_id=other(i)[1], device_id_type=MESH)
        return 0

    lax.fori_loop(1, n, greet, 0)

    bf = jnp.bfloat16
    f32 = jnp.float32
    tall = lax.broadcasted_iota(jnp.int32, (128, 128), 0).astype(f32)
    wide = lax.broadcasted_iota(jnp.int32, (128, 128), 1).astype(f32)
    eight = lax.broadcasted_iota(jnp.int32, (8, 128), 0).astype(f32)

    def hot(rows, row):
        return jnp.where(rows == row, 1.0, 0.0)

    cell, slot = cell_ref[...], slot_ref[...]
    owner = (slot // 1024).astype(f32)
    row = slot % 1024
    row_hi, row_lo = (row // 128 + 1).astype(f32), (row % 128).astype(f32)
    cell_x, cell_y = (cell // 128).astype(f32), (cell % 128).astype(f32)
    by_cell = jnp.zeros((24, 128), f32)
    for b in range(8):
        here = hot(eight, cell_x[b : b + 1])
        left = jnp.concatenate([here * w[b : b + 1] for w in (owner, row_hi, row_lo)], 0)
        by_cell = by_cell + nt(left.astype(bf), hot(tall, cell_y[b : b + 1]).astype(bf))
    owner, row_hi, row_lo = by_cell[0:8], by_cell[8:16], by_cell[16:24]

    before = jnp.where(tall < wide, 1.0, 0.0).astype(bf)
    ones = jnp.ones((128, 128), bf)
    seen = jnp.zeros((128, 128), f32)
    slot_k = lax.broadcasted_iota(jnp.int32, (MOST, 128), 0).astype(f32)
    for x in range(8):
        mine = hot(tall, owner[x : x + 1])
        mine_b = mine.astype(bf)
        a_ref[:, x * 128 : (x + 1) * 128] = mine_b
        count = jnp.dot(mine_b, before, preferred_element_type=f32) + jnp.dot(
            seen.astype(bf), ones, preferred_element_type=f32
        )
        seen = seen + mine
        place = jnp.sum(mine * count, axis=0, keepdims=True)
        at_k = hot(slot_k, place)
        cols = slice(x * 128, (x + 1) * 128)
        for f in range(COEF):
            val = v_ref[f * 8 + x : f * 8 + x + 1, :]
            hi = val.astype(bf).astype(f32)
            lo = val - hi
            m_ref[f * MOST : (f + 1) * MOST, cols] = (at_k * hi).astype(bf)
            m_ref[(COEF + f) * MOST : (COEF + f + 1) * MOST, cols] = (at_k * lo).astype(bf)
        base = 2 * COEF * MOST
        m_ref[base : base + MOST, cols] = (at_k * row_hi[x : x + 1]).astype(bf)
        m_ref[base + MOST : base + 2 * MOST, cols] = (at_k * row_lo[x : x + 1]).astype(bf)
        m_ref[base + 2 * MOST : base + 4 * MOST, cols] = jnp.zeros((2 * MOST, 128), bf)

    for g in range(4):
        hi = nt(a_ref[...], m_ref[g * 128 : (g + 1) * 128, :])
        lo = nt(a_ref[...], m_ref[512 + g * 128 : 512 + (g + 1) * 128, :])
        snd[g] = hi + lo
    snd[4] = nt(a_ref[...], m_ref[1024:1152, :])

    pl.semaphore_wait(barrier, n - 1)
    mine = pl.ds(me, 1)
    own = pltpu.make_async_copy(snd.at[:, mine, :], rcv.at[:, mine, :], local_sem)
    own.start()

    def send(i, _):
        t, device = other(i)
        pltpu.make_async_remote_copy(
            snd.at[:, pl.ds(t, 1), :], rcv.at[:, mine, :], send_sem, recv_sem, device_id=device, device_id_type=MESH
        ).start()
        return 0

    lax.fori_loop(1, n, send, 0)
    own.wait()
    rest = pl.ds(0, n - 1)
    pltpu.make_async_remote_copy(
        snd.at[:, rest, :], rcv.at[:, rest, :], send_sem, recv_sem, device_id=other(1)[1], device_id_type=MESH
    ).wait()

    where = rcv[4].T
    vals = [rcv[g].T for g in range(4)]
    for k in range(MOST):
        cols = slice(k * 128, (k + 1) * 128)
        rhs[:, cols] = hot(tall, where[MOST + k : MOST + k + 1]).astype(bf)
        at_hi = hot(eight + 1.0, where[k : k + 1])
        for f in range(COEF):
            at = (f % 4) * MOST + k
            part = at_hi * vals[f // 4][at : at + 1]
            hi = part.astype(bf)
            lhs[f * 8 : f * 8 + 8, cols] = part
    whole = lhs[...]
    hi = whole.astype(bf)
    lo = (whole - hi.astype(f32)).astype(bf)
    out_ref[...] = nt(hi, rhs[...]) + nt(lo, rhs[...])


def solution(mesh):
    n_gx, n_gy = mesh.shape["gx"], mesh.shape["gy"]
    f32 = jnp.float32
    vmem = pl.BlockSpec(memory_space=pltpu.VMEM)
    smem = pl.BlockSpec(memory_space=pltpu.SMEM)
    dma = pltpu.SemaphoreType.DMA

    def local(enthalpy_start, tangent_start, labels, curve_parameters, pixel_cells, row_slot):
        e = enthalpy_start.reshape(64, 128)
        t = tangent_start.reshape(1024, 128)
        lab = labels.reshape(64, 128)
        e_end, t_end, v = pl.pallas_call(
            functools.partial(steps_kernel, n_gx, n_gy),
            out_shape=[
                jax.ShapeDtypeStruct((64, 128), f32),
                jax.ShapeDtypeStruct((1024, 128), f32),
                jax.ShapeDtypeStruct((128, 128), f32),
            ],
            in_specs=[vmem, vmem, vmem, smem],
            out_specs=[vmem, vmem, vmem],
            scratch_shapes=[
                pltpu.VMEM((128, 128), f32),
                pltpu.VMEM((2, 128, 128), f32),
                pltpu.VMEM((2, 1024, 128), f32),
                pltpu.VMEM((2, 72, 128), f32),
                pltpu.VMEM((3, 2, 72, 128), f32),
                pltpu.VMEM((2 * ALL, 8, 128), f32),
                pltpu.VMEM((ALL, 8, 128), f32),
                pltpu.VMEM((3 * ALL, 8, 128), f32),
                pltpu.VMEM((STEPS * ALL, 8, 128), f32),
                pltpu.VMEM((STEPS * COEF * ALL, 8, 128), f32),
                dma((2,)), dma((2,)), dma((8, 2)), dma((8, 2)), dma((2, 3, 2)), dma((2, 3, 2)),
            ],
            compiler_params=pltpu.CompilerParams(
                collective_id=0, has_side_effects=True, vmem_limit_bytes=48 * 2**20
            ),
            name="steps",
        )(e, t, lab, curve_parameters)
        rows = pl.pallas_call(
            functools.partial(rows_kernel, n_gx, n_gy),
            out_shape=jax.ShapeDtypeStruct((128, 128), f32),
            in_specs=[vmem, vmem, vmem],
            out_specs=vmem,
            scratch_shapes=[
                pltpu.VMEM((128, 1024), jnp.bfloat16),
                pltpu.VMEM((1152, 1024), jnp.bfloat16),
                pltpu.VMEM((5, 128, 128), f32),
                pltpu.VMEM((5, 128, 128), f32),
                pltpu.VMEM((128, 4096), f32),
                pltpu.VMEM((128, 4096), jnp.bfloat16),
                dma, dma, dma,
            ],
            compiler_params=pltpu.CompilerParams(
                collective_id=1, has_side_effects=True, vmem_limit_bytes=48 * 2**20
            ),
            name="rows",
        )(v, pixel_cells.reshape(8, 128), row_slot.reshape(8, 128))
        return (
            e_end.reshape(8, 8, 128),
            t_end.reshape(COEF, 8, 8, 128),
            rows.reshape(COEF, 1024),
        )

    in_specs = (
        P(None, "gx", "gy"),
        P(None, None, "gx", "gy"),
        P(None, "gx", "gy"),
        P(),
        P(("gx", "gy")),
        P(("gx", "gy")),
    )
    out_specs = (P(None, "gx", "gy"), P(None, None, "gx", "gy"), P(None, ("gx", "gy")))
    return jax.shard_map(local, mesh=mesh, in_specs=in_specs, out_specs=out_specs, check_vma=False)
```

time: 1070 us -> 62.9 us (0.06); the launches traced: 1050 us -> 62.6 us
  waiting for transfers between devices: 782 us -> 0 us
  starting transfers between devices: 111 us -> 0 us
  local copies, waits for them, and re-layouts: 86.2 us -> 5.95 us
  other arithmetic: 57.1 us -> 0 us
  Pallas kernels: 0 us -> 55.9 us
  between operations: 16 us -> 0.68 us
    reduce_scatter x1 -> x0, waiting for transfers between devices: 746 us -> none  [local(): lax.psum_scatter(dense_block, ('gx', 'gy'), scatter_dimension=1, tiled=True)]
    ppermute x36 -> x0, starting transfers between devices: 111 us -> none  [the longest x18 78.7 us: padded_2(): before = lax.ppermute(last, axis, up)]
    pallas_call x0 -> x2, Pallas kernels: none -> 55.9 us  [the longest x1 39.9 us: local(): pl.pallas_call(functools.partial(steps_kernel, n_gx, n_gy), out_shape=[ja...]
    scatter x2 -> x0, local copies, waits for them, and re-layouts: 38.6 us -> none  [local(): dense_block = jnp.zeros((parameter_total, devices * pixel_count), jnp.flo...]
    ppermute x36 -> x0, waiting for transfers between devices: 36.4 us -> none  [the longest x18 35.9 us: padded_2(): after = lax.ppermute(leading, axis, down)]
    concatenate x26 -> x0, other arithmetic: 26 us -> none  [the longest x18 25.3 us: padded_2(): shard = jnp.concatenate([before, shard, after], axis=dim)]
    ppermute x16 -> x0, local copies, waits for them, and re-layouts: 23.6 us -> none  [the longest x8 13.4 us: padded_2(): before = lax.ppermute(last, axis, up)]
    add x26 -> x0, other arithmetic: 19.5 us -> none  [the longest x8 14 us: spread(): net_flow = net_flow + weight[None] * (other - sensitivity_matrix)]
  transfers between devices with their start and end apart: 37 -> 0, of which waited for: 12 -> 0; matrix products, arithmetic and copies ran while one was open for 2% -> 0% of each run, Pallas kernels for 0% -> 0%
where the time goes in v1:
time: 62.9 us; the launch traced here: 62.6 us
  Pallas kernels  55.9 us (89%)
  local copies, waits for them, and re-layouts  5.95 us (9%)
  between operations  0.68 us (1%)
    pallas_call x1, Pallas kernels, local(): pl.pallas_call(functools.partial(steps_kernel, n_gx, n_gy), out_shape=[ja...  39.9 us
    pallas_call x1, Pallas kernels, local(): pl.pallas_call(functools.partial(rows_kernel, n_gx, n_gy), out_shape=jax....  16 us
    unnamed x14, local copies, waits for them, and re-layouts  5.3 us

profile of v1, /device:TPU:1, one launch (start us, length us, event | category | flops | bytes accessed | tf_op | source)
XLA Modules:
  0.0 62.6 jit_solution(17849615491236392236)
XLA Ops:
  0.6 0.0 copy-start.5
  0.6 0.6 %copy-done.5 = f32[16]{0:T(128)S(1)} copy-done((f32[16]{0:T(128)S(1)}, f32[16]{0:T(128)}, u32[]{:S(2)}) %copy-start.5) | copy-done | bytes 88
  1.3 0.0 copy-start
  1.3 1.0 %copy-done = f32[16,8,8,128]{3,2,1,0:T(8,128)S(1)} copy-done((f32[16,8,8,128]{3,2,1,0:T(8,128)S(1)}, f32[16,8,8,128]{3,2,1,0:T(8,128)}, u32[]{:S(2)}) %copy-start) | copy-done | bytes 524312
  2.3 0.0 copy-start.1
  2.3 0.8 %copy-done.1 = f32[8,8,128]{2,1,0:T(8,128)S(1)} copy-done((f32[8,8,128]{2,1,0:T(8,128)S(1)}, f32[8,8,128]{2,1,0:T(8,128)}, u32[]{:S(2)}) %copy-start.1) | copy-done | bytes 32792
  3.1 0.0 copy-start.2
  3.1 0.8 %copy-done.2 = s32[8,8,128]{2,1,0:T(8,128)S(1)} copy-done((s32[8,8,128]{2,1,0:T(8,128)S(1)}, s32[8,8,128]{2,1,0:T(8,128)}, u32[]{:S(2)}) %copy-start.2) | copy-done | bytes 32792
  3.8 39.9 %steps.1 = (f32[64,128]{1,0:T(8,128)S(1)}, f32[1024,128]{1,0:T(8,128)S(1)}, f32[128,128]{1,0:T(8,128)S(1)}) custom-call(f32[64,128]{1,0:T(8,128)S(1)} %bitcast.10, f32[1024,128]{1,0:T(8,128)S(1)} %bitcast.7, s32[64,128]{1,0:T(8,128)S(1)} %bitcast.11, f32[16]{0:T(128)S(1)} %copy-done.5), custom_call_target="tpu_custom_call" | custom-call | tf_op jit(solution)/shard_map/steps/pallas_call | solution.py:451
  43.8 0.0 copy-start.4
  43.8 0.0 copy-start.3
  43.8 0.7 %copy-done.4 = s32[1024]{0:T(1024)S(1)} copy-done((s32[1024]{0:T(1024)S(1)}, s32[1024]{0:T(1024)}, u32[]{:S(2)}) %copy-start.4) | copy-done | bytes 4120
  44.5 0.0 copy-done.3
  44.5 16.0 %rows.1 = f32[128,128]{1,0:T(8,128)S(1)} custom-call(f32[128,128]{1,0:T(8,128)S(1)} %get-tuple-element.8.v_ref, s32[8,128]{1,0:T(8,128)S(1)} %bitcast.12, s32[8,128]{1,0:T(8,128)S(1)} %bitcast.13), custom_call_target="tpu_custom_call" | custom-call | tf_op jit(solution)/shard_map/rows/pallas_call | solution.py:478
  60.5 0.6 %reshape.37 = f32[16,1024]{1,0:T(8,128)} reshape(f32[128,128]{1,0:T(8,128)S(1)} %rows.1) | data formatting | bytes 131072 | tf_op jit(solution)/shard_map/reshape | solution.py:500
  61.2 0.6 copy.11
  61.8 0.8 %copy.12 = f32[16,8,8,128]{3,2,1,0:T(8,128)} copy(f32[16,8,8,128]{3,2,1,0:T(8,128)S(1)} %bitcast.8) | data formatting | bytes 1048576
Async XLA Ops:
  0.6 0.7 %copy-start.5 = (f32[16]{0:T(128)S(1)}, f32[16]{0:T(128)}, u32[]{:S(2)}) copy-start(f32[16]{0:T(128)} %coef_ref.1) | copy-start | bytes 196
  1.3 1.0 %copy-start = (f32[16,8,8,128]{3,2,1,0:T(8,128)S(1)}, f32[16,8,8,128]{3,2,1,0:T(8,128)}, u32[]{:S(2)}) copy-start(f32[16,8,8,128]{3,2,1,0:T(8,128)} %param.7) | copy-start | bytes 1572868
  2.3 0.8 %copy-start.1 = (f32[8,8,128]{2,1,0:T(8,128)S(1)}, f32[8,8,128]{2,1,0:T(8,128)}, u32[]{:S(2)}) copy-start(f32[8,8,128]{2,1,0:T(8,128)} %param.6) | copy-start | bytes 98308
  3.1 0.8 %copy-start.2 = (s32[8,8,128]{2,1,0:T(8,128)S(1)}, s32[8,8,128]{2,1,0:T(8,128)}, u32[]{:S(2)}) copy-start(s32[8,8,128]{2,1,0:T(8,128)} %param.8) | copy-start | bytes 98308
  43.8 0.7 %copy-start.4 = (s32[1024]{0:T(1024)S(1)}, s32[1024]{0:T(1024)}, u32[]{:S(2)}) copy-start(s32[1024]{0:T(1024)} %param.11) | copy-start | bytes 12292
  43.8 0.7 %copy-start.3 = (s32[1024]{0:T(1024)S(1)}, s32[1024]{0:T(1024)}, u32[]{:S(2)}) copy-start(s32[1024]{0:T(1024)} %param.10) | copy-start | bytes 12292

commit v2 on v0

v2 whole, which is shorter than its diff:
```python
import functools
import math

import jax
import jax.numpy as jnp
from jax import lax
from jax.experimental import pallas as pl
from jax.experimental.pallas import tpu as pltpu
from jax.sharding import PartitionSpec as P

COEF = 16
RATE = 0.15
WIDTH = 0.3
ROOT = math.sqrt(math.log2(math.e))
KNOTS = [-2.0 + 0.25 * (j + 0.5) for j in range(COEF)]

DEEP = 4
ROUNDS = 2
MAIN = 16
STRIP = 4
ALL = MAIN + STRIP
ENTH = COEF
MOST = 32
MESH = pl.DeviceIdType.MESH
F32 = jnp.float32
BF16 = jnp.bfloat16


def lanes():
    return lax.broadcasted_iota(jnp.int32, (8, 128), 1)


def turn(v, shift, axis):
    shift = shift % v.shape[axis]
    return v if shift == 0 else pltpu.roll(v, shift, axis)


def place(v, mask, piece):
    return piece if v is None else jnp.where(mask, piece, v)


def own_strips(rows):
    lane = lanes()
    out = []
    for g in range(STRIP):
        v = None
        for c in (1, 2):
            row = rows[4 * (c - 1) + g]
            v = place(v, lane // 16 == c, turn(row, 16 * c + 4, 1))
            v = place(v, lane // 16 == 4 + c, turn(row, 64 + 16 * c - 116, 1))
        out.append(v)
    return out


def pack_edges(strips, it, last, first):
    lane = lanes()
    for g in range(STRIP):
        here = (lane // 32 == g) & (lane % 16 // 4 == it)
        last = place(last, here, turn(strips[g], 32 * g + 4 * it - 88, 1))
        first = place(first, here, turn(strips[g], 32 * g + 4 * it - 20, 1))
    return last, first


def full_strips(own, low, high, before, after, it):
    lane = lanes()
    block, inside = lane // 16, lane % 16
    out = []
    for g in range(STRIP):
        v = own[g]
        v = place(v, block == 0, turn(low[g], 4, 1))
        v = place(v, block == 3, turn(high[g], 52, 1))
        v = place(v, block == 4, turn(low[g], -52, 1))
        v = place(v, block == 7, turn(high[g], -4, 1))
        at = 32 * g + 4 * it
        first, last = inside < 4, inside >= 12
        v = place(v, ((block == 1) | (block == 2)) & first, turn(before[1], 16 - at, 1))
        v = place(v, (block == 0) & first, turn(before[0], -16 - at, 1))
        v = place(v, (block == 3) & first, turn(before[2], 48 - at, 1))
        v = place(v, ((block == 5) | (block == 6)) & last, turn(after[1], 92 - at, 1))
        v = place(v, (block == 4) & last, turn(after[0], 60 - at, 1))
        v = place(v, (block == 7) & last, turn(after[2], 124 - at, 1))
        out.append(v)
    return out


def merge(state):
    lane = lanes()
    out = []
    for x in range(8):
        c, g = 1 + x // 4, x % 4
        v = jnp.where(lane < 4, turn(state[MAIN + g], -(16 * c + 4), 1), state[x + DEEP])
        out.append(jnp.where(lane >= 124, turn(state[MAIN + g], 124 - (72 + 16 * c), 1), v))
    return out


def advance(step, state, temp, wx, wy, wz):
    new = list(state)

    def own(i, t):
        fy = wy(i) * (turn(t, -1, 1) - t)
        fz = wz(i) * (turn(t, -1, 0) - t)
        return (fy - turn(fy, 1, 1)) + (fz - turn(fz, 1, 0))

    lo, hi = step, MAIN - step
    t = temp(lo)
    t_next = temp(lo + 1)
    flux = wx(lo) * (t_next - t)
    for i in range(lo + 1, hi - 1):
        t, t_next = t_next, temp(i + 1)
        below, flux = flux, wx(i) * (t_next - t)
        new[i] = state[i] + ((flux - below) + own(i, t))
    ts = [temp(i) for i in range(MAIN, ALL)]
    fluxes = [wx(MAIN + g) * ((ts[g + 1] if g < STRIP - 1 else turn(ts[0], -16, 1)) - ts[g]) for g in range(STRIP)]
    for g in range(STRIP):
        below = fluxes[g - 1] if g > 0 else turn(fluxes[-1], 16, 1)
        new[MAIN + g] = state[MAIN + g] + ((fluxes[g] - below) + own(MAIN + g, ts[g]))
    return new


def nt(a, b):
    return lax.dot_general(a, b, (((1,), (1,)), ((), ())), preferred_element_type=F32)


def hot(rows, row):
    return jnp.where(rows == row, 1.0, 0.0)


def kernel(
    n_gx, n_gy,
    e_ref, t_ref, lab_ref, coef_ref, cell_ref, slot_ref,
    e_out, t_out, rows_out,
    e_in, lab_in, own, mid, hx0, hx1, pk, hp, own_st, est, tst, wst, sl, bump,
    a_ref, atk, tab, m_ref, snd, rcv, lhs, rhs,
    in_sem, out_sem, x_send, x_recv, p_send, p_recv, line_sem, local_sem, all_send, all_recv,
):
    n = n_gx * n_gy
    gx, gy = lax.axis_index("gx"), lax.axis_index("gy")
    me = gx * n_gy + gy

    def at(dx, dy):
        return lax.rem(gx + dx + n_gx, n_gx), lax.rem(gy + dy + n_gy, n_gy)

    corners = [(dx, dy) for dx in (0, -1, 1) for dy in (-1, 1)]
    line = [(dx, 0) for dx in range(1, n_gx)]
    greeted = line + [(0, dy) for dy in range(1, n_gy)] + [c for c in corners if c[0] != 0]
    barrier = pltpu.get_barrier_semaphore()
    for dx, dy in greeted:
        pl.semaphore_signal(barrier, inc=1, device_id=at(dx, dy), device_id_type=MESH)

    def load_e():
        return pltpu.make_async_copy(e_ref, e_in, in_sem.at[8])

    def load_lab():
        return pltpu.make_async_copy(lab_ref, lab_in, in_sem.at[9])

    def load_t(x):
        return pltpu.make_async_copy(t_ref.at[:, x, :], own.at[x, pl.ds(0, 128), :], in_sem.at[x])

    load_e().start()
    load_lab().start()
    for x in range(8):
        load_t(x).start()
    load_e().wait()
    load_lab().wait()
    pair = [[], []]
    for x in range(8):
        pair[0].append(e_in[pl.ds(x, 8, stride=8), :])
        pair[1].append(jnp.where(lab_in[pl.ds(x, 8, stride=8), :] == 1, 1.0, 0.0))
        for k in range(2):
            own[x, (ENTH + k) * 8 : (ENTH + k + 1) * 8, :] = pair[k][x]

    halos = (hx0, hx1)

    def send_x(r, q, d):
        part = pl.ds(q * 32, 32) if not isinstance(q, int) or q < 4 else pl.ds(128, 16 if r == 0 else 8)
        source = own if r == 0 else mid
        return pltpu.make_async_remote_copy(
            source.at[pl.ds(DEEP - DEEP * d, DEEP), part, :], halos[r].at[d, :, part, :],
            x_send.at[r, q, d], x_recv.at[r, q, d], device_id=at(1 - 2 * d, 0), device_id_type=MESH,
        )

    def send_p(r, group, dx, dy):
        part = pl.ds(group * 16, 16) if group < 2 else pl.ds(32, 8)
        side = 0 if dy == 1 else 1
        return pltpu.make_async_remote_copy(
            pk.at[r, side, part], hp.at[r, 1 - dx, side, part],
            p_send.at[r, group, dx + 1, side], p_recv.at[r, group, 1 - dx, side],
            device_id=at(dx, dy), device_id_type=MESH,
        )

    def store_pack(r, q, last, first):
        to = pl.ds(pl.multiple_of(q * 8, 8), 8)
        pk[r, 0, to, :] = last
        pk[r, 1, to, :] = first

    def store_strips(item, strips):
        for g in range(STRIP):
            own_st[item * STRIP + g] = strips[g]

    last = first = None
    for k in range(2):
        strips = own_strips(pair[k])
        store_strips(ENTH + k, strips)
        last, first = pack_edges(strips, k, last, first)
    store_pack(0, 4, last, first)

    pl.semaphore_wait(barrier, len(greeted))
    for d in range(2):
        send_x(0, 4, d).start()
    for dx, dy in corners:
        send_p(0, 2, dx, dy).start()
    for dx, dy in line:
        pl.semaphore_signal(line_sem, inc=1, device_id=at(dx, dy), device_id_type=MESH)
    for x in range(8):
        load_t(x).wait()
    for q in range(4):
        for d in range(2):
            send_x(0, q, d).start()

    def own_rows(ref, item):
        part = pl.ds(pl.multiple_of(item * 8, 8), 8)
        return [ref[x, part, :] for x in range(8)]

    def pack_quad(q, _):
        last = first = None
        for it in range(4):
            strips = own_strips(own_rows(own, q * 4 + it))
            store_strips(q * 4 + it, strips)
            last, first = pack_edges(strips, it, last, first)
        store_pack(0, q, last, first)
        return 0

    lax.fori_loop(0, 4, pack_quad, 0)
    for group in range(2):
        for dx, dy in corners:
            send_p(0, group, dx, dy).start()

    tall = lax.broadcasted_iota(jnp.int32, (128, 128), 0).astype(F32)
    wide = lax.broadcasted_iota(jnp.int32, (128, 128), 1).astype(F32)
    eight = lax.broadcasted_iota(jnp.int32, (8, 128), 0).astype(F32)
    cell, slot = cell_ref[...], slot_ref[...]
    owner = (slot // 1024).astype(F32)
    row = slot % 1024
    row_hi, row_lo = (row // 128 + 1).astype(F32), (row % 128).astype(F32)
    cell_x, cell_y = (cell // 128).astype(F32), (cell % 128).astype(F32)
    by_cell = jnp.zeros((24, 128), F32)
    for b in range(8):
        here = hot(eight, cell_x[b : b + 1])
        left = jnp.concatenate([here * w[b : b + 1] for w in (owner, row_hi, row_lo)], 0)
        by_cell = by_cell + nt(left.astype(BF16), hot(tall, cell_y[b : b + 1]).astype(BF16))
    owner, row_hi, row_lo = by_cell[0:8], by_cell[8:16], by_cell[16:24]
    earlier = jnp.where(tall < wide, 1.0, 0.0).astype(BF16)
    ones = jnp.ones((128, 128), BF16)
    seen = jnp.zeros((128, 128), F32)
    slot_k = lax.broadcasted_iota(jnp.int32, (MOST, 128), 0).astype(F32)
    for x in range(8):
        cols = slice(x * 128, (x + 1) * 128)
        mine = hot(tall, owner[x : x + 1])
        mine_b = mine.astype(BF16)
        a_ref[:, cols] = mine_b
        count = jnp.dot(mine_b, earlier, preferred_element_type=F32) + jnp.dot(
            seen.astype(BF16), ones, preferred_element_type=F32
        )
        seen = seen + mine
        at_k = hot(slot_k, jnp.sum(mine * count, axis=0, keepdims=True))
        atk[x] = at_k
        tab[0:MOST, cols] = (at_k * row_hi[x : x + 1]).astype(BF16)
        tab[MOST : 2 * MOST, cols] = (at_k * row_lo[x : x + 1]).astype(BF16)
        tab[2 * MOST : 4 * MOST, cols] = jnp.zeros((2 * MOST, 128), BF16)
    snd[4] = nt(a_ref[...], tab[...])

    def halo_rows(r, d, item):
        part = pl.ds(pl.multiple_of(item * 8, 8), 8)
        return [halos[r][d, x, part, :] for x in range(DEEP)]

    def all_rows(r, item, q, it):
        low, high = halo_rows(r, 0, item), halo_rows(r, 1, item)
        main = low + own_rows(own if r == 0 else mid, item) + high
        part = pl.ds(pl.multiple_of(q * 8, 8), 8)
        before = [hp[r, k, 0, part, :] for k in range(3)]
        after = [hp[r, k, 1, part, :] for k in range(3)]
        strips = [own_st[item * STRIP + g] for g in range(STRIP)]
        return main + full_strips(strips, low, high, before, after, it)

    def wait_e(r):
        for d in range(2):
            send_x(r, 4, d).wait()
        for dx, dy in corners:
            send_p(r, 2, dx, dy).wait()

    wait_e(0)
    pcm = all_rows(0, ENTH + 1, 4, 1)
    for i in range(ALL):
        est[ALL + i] = pcm[i]

    lane = lanes()
    block, inside = lane // 16, lane % 16
    layer = lax.broadcasted_iota(jnp.int32, (8, 128), 0)
    open_x0 = jnp.where(gx == 0, 0.0, 1.0)
    open_x1 = jnp.where(gx == n_gx - 1, 0.0, 1.0)
    open_y0 = jnp.where(gy == 0, 0.0, 1.0)
    open_y1 = jnp.where(gy == n_gy - 1, 0.0, 1.0)
    cond = [1.0 - 0.5 * p for p in pcm]

    def face(a, b):
        return (2.0 * RATE) * a * b / (a + b)

    edge_y = jnp.where((block < 4) & (inside == 3), open_y0, 1.0)
    edge_y = jnp.where((block >= 4) & (inside == 11), open_y1, edge_y)
    edge_x = jnp.where((block == 0) | (block == 4), open_x0, 1.0)
    edge_x = jnp.where((block == 2) | (block == 6), open_x1, edge_x)
    for i in range(ALL):
        c = cond[i]
        if i == MAIN - 1:
            up = c
        elif i == ALL - 1:
            up = turn(cond[MAIN], -16, 1)
        else:
            up = cond[i + 1]
        wx = face(c, up)
        if i == 3:
            wx = wx * open_x0
        if i == 11:
            wx = wx * open_x1
        if i == ALL - 1:
            wx = wx * edge_x
        wst[i] = wx
        wy = face(c, turn(c, -1, 1))
        wst[ALL + i] = wy * edge_y if i >= MAIN else wy
        wst[2 * ALL + i] = jnp.where(layer == 7, 0.0, face(c, turn(c, -1, 0)))

    weights = (lambda i: wst[i], lambda i: wst[ALL + i], lambda i: wst[2 * ALL + i])

    def shape_row(s, i):
        e = est[i]
        p = est[ALL + i] > 0
        scaled = jnp.where(p, e, 100.0) * (ROOT / WIDTH)
        total = jnp.zeros((8, 128), F32)
        slope = jnp.zeros((8, 128), F32)
        for j in range(COEF):
            v = scaled - KNOTS[j] * (ROOT / WIDTH)
            b = jnp.exp2(-(v * v))
            bump[(s * COEF + j) * ALL + i] = b
            cb = coef_ref[j] * b
            total = total + cb
            slope = slope + v * cb
        half = jnp.where(p, 1.0, 0.5)
        tst[i] = half * e + total
        sl[s * ALL + i] = half - (2.0 / (WIDTH * ROOT)) * slope

    def shape_rows(s, lo, hi):
        for i in range(lo, lo + (hi - lo) % 4):
            shape_row(s, i)
        lo += (hi - lo) % 4

        def four(k, _):
            for i in range(4):
                shape_row(s, lo + k * 4 + i)
            return 0

        lax.fori_loop(0, (hi - lo) // 4, four, 0)

    def enthalpy(r):
        start = all_rows(r, ENTH, 4, 0)
        for i in range(ALL):
            est[i] = start[i]
        for s in range(DEEP):
            shape_rows(s, s, MAIN - s)
            shape_rows(s, MAIN, ALL)
            state = [est[i] for i in range(ALL)]
            new = advance(s, state, lambda i: tst[i], *weights)
            for i in range(ALL):
                if new[i] is not state[i]:
                    est[i] = new[i]
        state = [est[i] for i in range(ALL)]
        done = merge(state)
        for x in range(8):
            mid[x, ENTH * 8 : ENTH * 8 + 8, :] = done[x]
        if r == 0:
            store_strips(ENTH, state[MAIN:])
            last, first = pack_edges(state[MAIN:], 0, None, None)
            store_pack(1, 4, last, first)

    def tangents(r, q):
        last = first = None
        for it in range(4):
            j = q * 4 + it
            state = all_rows(r, j, q, it)
            for s in range(DEEP):
                def temp(i, s=s, state=state):
                    return sl[s * ALL + i] * state[i] + bump[(s * COEF + j) * ALL + i]

                state = advance(s, state, temp, *weights)
            done = merge(state)
            part = pl.ds(pl.multiple_of(j * 8, 8), 8)
            for x in range(8):
                mid[x, part, :] = done[x]
            if r == 0:
                store_strips(j, state[MAIN:])
                last, first = pack_edges(state[MAIN:], it, last, first)
        if r == 0:
            store_pack(1, q, last, first)

    enthalpy(0)
    for d in range(2):
        send_x(1, 4, d).start()
    for dx, dy in corners:
        send_p(1, 2, dx, dy).start()
    for group in range(2):
        for dx, dy in corners:
            send_p(0, group, dx, dy).wait()

    def first_round(q, _):
        for d in range(2):
            send_x(0, q, d).wait()
        tangents(0, q)
        for d in range(2):
            send_x(1, q, d).start()
        for group in range(2):
            @pl.when(q == 2 * group + 1)
            def _():
                for dx, dy in corners:
                    send_p(1, group, dx, dy).start()
        return 0

    lax.fori_loop(0, 4, first_round, 0)
    wait_e(1)
    enthalpy(1)

    def second_round(q, _):
        for group in range(2):
            @pl.when(q == 2 * group)
            def _():
                for dx, dy in corners:
                    send_p(1, group, dx, dy).wait()
        for d in range(2):
            send_x(1, q, d).wait()
        tangents(1, q)
        return 0

    lax.fori_loop(0, 4, second_round, 0)

    def store_t(x):
        return pltpu.make_async_copy(mid.at[x, pl.ds(0, 128), :], t_out.at[:, x, :], out_sem.at[x])

    def store_e():
        return pltpu.make_async_copy(e_in, e_out, out_sem.at[8])

    for x in range(8):
        e_in[pl.ds(x, 8, stride=8), :] = mid[x, ENTH * 8 : ENTH * 8 + 8, :]
    store_e().start()
    for x in range(8):
        store_t(x).start()

    def top(item):
        v = jnp.broadcast_to(mid[0, item * 8 + 7 : item * 8 + 8, :], (8, 128))
        for x in range(1, 8):
            v = jnp.where(eight == x, mid[x, item * 8 + 7 : item * 8 + 8, :], v)
        return v

    p7 = jnp.where(lab_in[56:64, :] == 1, 1.0, 0.0) > 0
    scaled = jnp.where(p7, top(ENTH), 100.0) * (ROOT / WIDTH)
    slope = jnp.zeros((8, 128), F32)
    bumps = []
    for j in range(COEF):
        v = scaled - KNOTS[j] * (ROOT / WIDTH)
        b = jnp.exp2(-(v * v))
        bumps.append(b)
        slope = slope + v * (coef_ref[j] * b)
    slope = jnp.where(p7, 1.0, 0.5) - (2.0 / (WIDTH * ROOT)) * slope
    for f in range(COEF):
        val = slope * top(f) + bumps[f]
        hi = val.astype(BF16).astype(F32)
        lo = val - hi
        for x in range(8):
            cols = slice(x * 128, (x + 1) * 128)
            at_k = atk[x]
            m_ref[f * MOST : (f + 1) * MOST, cols] = (at_k * hi[x : x + 1]).astype(BF16)
            m_ref[(COEF + f) * MOST : (COEF + f + 1) * MOST, cols] = (at_k * lo[x : x + 1]).astype(BF16)
    for g in range(4):
        hi = nt(a_ref[...], m_ref[g * 128 : (g + 1) * 128, :])
        lo = nt(a_ref[...], m_ref[512 + g * 128 : 512 + (g + 1) * 128, :])
        snd[g] = hi + lo

    pl.semaphore_wait(line_sem, len(line))
    mine = pl.ds(me, 1)
    keep = pltpu.make_async_copy(snd.at[:, mine, :], rcv.at[:, mine, :], local_sem)
    keep.start()

    def send_rows(i, _):
        t = lax.rem(me + i, n)
        pltpu.make_async_remote_copy(
            snd.at[:, pl.ds(t, 1), :], rcv.at[:, mine, :], all_send, all_recv,
            device_id=(t // n_gy, lax.rem(t, n_gy)), device_id_type=MESH,
        ).start()
        return 0

    lax.fori_loop(1, n, send_rows, 0)
    keep.wait()
    rest = pl.ds(0, n - 1)
    pltpu.make_async_remote_copy(
        snd.at[:, rest, :], rcv.at[:, rest, :], all_send, all_recv, device_id=at(1, 0), device_id_type=MESH
    ).wait()

    where = rcv[4].T
    vals = [rcv[g].T for g in range(4)]
    for k in range(MOST):
        cols = slice(k * 128, (k + 1) * 128)
        rhs[:, cols] = hot(tall, where[MOST + k : MOST + k + 1]).astype(BF16)
        at_hi = hot(eight + 1.0, where[k : k + 1])
        for f in range(COEF):
            at_f = (f % 4) * MOST + k
            lhs[f * 8 : f * 8 + 8, cols] = at_hi * vals[f // 4][at_f : at_f + 1]
    whole = lhs[...]
    hi = whole.astype(BF16)
    lo = (whole - hi.astype(F32)).astype(BF16)
    rows_out[...] = nt(hi, rhs[...]) + nt(lo, rhs[...])
    store_e().wait()
    for x in range(8):
        store_t(x).wait()


def solution(mesh):
    n_gx, n_gy = mesh.shape["gx"], mesh.shape["gy"]
    vmem = pl.BlockSpec(memory_space=pltpu.VMEM)
    smem = pl.BlockSpec(memory_space=pltpu.SMEM)
    hbm = pl.BlockSpec(memory_space=pl.ANY)
    dma = pltpu.SemaphoreType.DMA

    def tiles(*shape):
        return pltpu.VMEM((*shape, 8, 128), F32)

    def local(enthalpy_start, tangent_start, labels, curve_parameters, pixel_cells, row_slot):
        e_end, t_end, rows = pl.pallas_call(
            functools.partial(kernel, n_gx, n_gy),
            out_shape=[
                jax.ShapeDtypeStruct((64, 128), F32),
                jax.ShapeDtypeStruct((128, 8, 128), F32),
                jax.ShapeDtypeStruct((128, 128), F32),
            ],
            in_specs=[hbm, hbm, hbm, smem, vmem, vmem],
            out_specs=[hbm, hbm, vmem],
            scratch_shapes=[
                pltpu.VMEM((64, 128), F32),
                pltpu.VMEM((64, 128), jnp.int32),
                pltpu.VMEM((8, 144, 128), F32),
                pltpu.VMEM((8, 136, 128), F32),
                pltpu.VMEM((2, DEEP, 144, 128), F32),
                pltpu.VMEM((2, DEEP, 136, 128), F32),
                pltpu.VMEM((ROUNDS, 2, 40, 128), F32),
                pltpu.VMEM((ROUNDS, 3, 2, 40, 128), F32),
                tiles((COEF + 2) * STRIP),
                tiles(2 * ALL),
                tiles(ALL),
                tiles(3 * ALL),
                tiles(DEEP * ALL),
                tiles(DEEP * COEF * ALL),
                pltpu.VMEM((128, 1024), BF16),
                pltpu.VMEM((8, MOST, 128), F32),
                pltpu.VMEM((128, 1024), BF16),
                pltpu.VMEM((1024, 1024), BF16),
                pltpu.VMEM((5, 128, 128), F32),
                pltpu.VMEM((5, 128, 128), F32),
                pltpu.VMEM((128, 4096), F32),
                pltpu.VMEM((128, 4096), BF16),
                dma((10,)), dma((9,)),
                dma((ROUNDS, 5, 2)), dma((ROUNDS, 5, 2)),
                dma((ROUNDS, 3, 3, 2)), dma((ROUNDS, 3, 3, 2)),
                pltpu.SemaphoreType.REGULAR, dma, dma, dma,
            ],
            compiler_params=pltpu.CompilerParams(
                collective_id=0, has_side_effects=True, vmem_limit_bytes=48 * 2**20
            ),
            name="steps",
        )(
            enthalpy_start.reshape(64, 128), tangent_start.reshape(128, 8, 128), labels.reshape(64, 128),
            curve_parameters, pixel_cells.reshape(8, 128), row_slot.reshape(8, 128),
        )
        return (
            e_end.reshape(8, 8, 128),
            t_end.reshape(COEF, 8, 8, 128),
            rows.reshape(COEF, 1024),
        )

    in_specs = (
        P(None, "gx", "gy"),
        P(None, None, "gx", "gy"),
        P(None, "gx", "gy"),
        P(),
        P(("gx", "gy")),
        P(("gx", "gy")),
    )
    out_specs = (P(None, "gx", "gy"), P(None, None, "gx", "gy"), P(None, ("gx", "gy")))
    return jax.shard_map(local, mesh=mesh, in_specs=in_specs, out_specs=out_specs, check_vma=False)
```

time: 1070 us -> 53.5 us (0.05); the launches traced: 1050 us -> 53.2 us
  waiting for transfers between devices: 782 us -> 0 us
  starting transfers between devices: 111 us -> 0 us
  local copies, waits for them, and re-layouts: 86.2 us -> 5.29 us
  other arithmetic: 57.1 us -> 0 us
  Pallas kernels: 0 us -> 47.2 us
  between operations: 16 us -> 0.67 us
    reduce_scatter x1 -> x0, waiting for transfers between devices: 746 us -> none  [local(): lax.psum_scatter(dense_block, ('gx', 'gy'), scatter_dimension=1, tiled=True)]
    ppermute x36 -> x0, starting transfers between devices: 111 us -> none  [the longest x18 78.7 us: padded_2(): before = lax.ppermute(last, axis, up)]
    pallas_call x0 -> x1, Pallas kernels: none -> 47.2 us  [local(): pl.pallas_call(functools.partial(kernel, n_gx, n_gy), out_shape=[jax.Shap...]
    scatter x2 -> x0, local copies, waits for them, and re-layouts: 38.6 us -> none  [local(): dense_block = jnp.zeros((parameter_total, devices * pixel_count), jnp.flo...]
    ppermute x36 -> x0, waiting for transfers between devices: 36.4 us -> none  [the longest x18 35.9 us: padded_2(): after = lax.ppermute(leading, axis, down)]
    concatenate x26 -> x0, other arithmetic: 26 us -> none  [the longest x18 25.3 us: padded_2(): shard = jnp.concatenate([before, shard, after], axis=dim)]
    ppermute x16 -> x0, local copies, waits for them, and re-layouts: 23.6 us -> none  [the longest x8 13.4 us: padded_2(): before = lax.ppermute(last, axis, up)]
    add x26 -> x0, other arithmetic: 19.5 us -> none  [the longest x8 14 us: spread(): net_flow = net_flow + weight[None] * (other - sensitivity_matrix)]
  transfers between devices with their start and end apart: 37 -> 0, of which waited for: 12 -> 0; matrix products, arithmetic and copies ran while one was open for 2% -> 0% of each run, Pallas kernels for 0% -> 0%
where the time goes in v2:
time: 53.5 us; the launch traced here: 53.2 us
  Pallas kernels  47.2 us (88%)
  local copies, waits for them, and re-layouts  5.29 us (10%)
  between operations  0.67 us (1%)
    pallas_call x1, Pallas kernels, local(): pl.pallas_call(functools.partial(kernel, n_gx, n_gy), out_shape=[jax.Shap...  47.2 us
    unnamed x14, local copies, waits for them, and re-layouts  4.64 us

profile of v2, /device:TPU:1, one launch (start us, length us, event | category | flops | bytes accessed | tf_op | source)
XLA Modules:
  0.0 53.2 jit_solution(1618309945740508051)
XLA Ops:
  0.6 0.0 copy-start.4
  0.6 0.0 copy-start.3
  0.7 0.0 copy-start.5
  0.7 0.7 %copy-done.4 = s32[1024]{0:T(1024)S(1)} copy-done((s32[1024]{0:T(1024)S(1)}, s32[1024]{0:T(1024)}, u32[]{:S(2)}) %copy-start.4) | copy-done | bytes 4120
  1.3 0.0 copy-done.3
  1.3 0.0 copy-done.5
  1.3 0.0 copy-start
  1.3 1.0 %copy-done = f32[16,8,8,128]{3,2,1,0:T(8,128)S(1)} copy-done((f32[16,8,8,128]{3,2,1,0:T(8,128)S(1)}, f32[16,8,8,128]{3,2,1,0:T(8,128)}, u32[]{:S(2)}) %copy-start) | copy-done | bytes 524312
  2.4 0.0 copy-start.1
  2.4 0.8 %copy-done.1 = f32[8,8,128]{2,1,0:T(8,128)S(1)} copy-done((f32[8,8,128]{2,1,0:T(8,128)S(1)}, f32[8,8,128]{2,1,0:T(8,128)}, u32[]{:S(2)}) %copy-start.1) | copy-done | bytes 32792
  3.1 0.0 copy-start.2
  3.1 0.8 %copy-done.2 = s32[8,8,128]{2,1,0:T(8,128)S(1)} copy-done((s32[8,8,128]{2,1,0:T(8,128)S(1)}, s32[8,8,128]{2,1,0:T(8,128)}, u32[]{:S(2)}) %copy-start.2) | copy-done | bytes 32792
  3.9 47.2 %steps.1 = (f32[64,128]{1,0:T(8,128)S(1)}, f32[128,8,128]{2,1,0:T(8,128)S(1)}, f32[128,128]{1,0:T(8,128)S(1)}) custom-call(f32[64,128]{1,0:T(8,128)S(1)} %bitcast.10, f32[128,8,128]{2,1,0:T(8,128)S(1)} %bitcast.7, s32[64,128]{1,0:T(8,128)S(1)} %bitcast.11, f32[16]{0:T(128)S(1)} %copy-done.5, s32[8,128]{1,0:T(8,128)S(1)} %bitcast.12, s32[8,128]{1,0:T(8,128)S(1)} %bitcast.13), custom_call_target="tpu_custom_call" | custom-call | tf_op jit(solution)/shard_map/steps/pallas_call | solution.py:534
  51.1 0.6 %reshape.37 = f32[16,1024]{1,0:T(8,128)} reshape(f32[128,128]{1,0:T(8,128)S(1)} %get-tuple-element.8) | data formatting | bytes 131072 | tf_op jit(solution)/shard_map/reshape | solution.py:582
  51.8 0.6 %copy.11 = f32[8,8,128]{2,1,0:T(8,128)} copy(f32[8,8,128]{2,1,0:T(8,128)S(1)} %bitcast.9) | data formatting | bytes 65536
  52.4 0.8 %copy.12 = f32[16,8,8,128]{3,2,1,0:T(8,128)} copy(f32[16,8,8,128]{3,2,1,0:T(8,128)S(1)} %bitcast.8) | data formatting | bytes 1048576
Async XLA Ops:
  0.6 0.7 %copy-start.4 = (s32[1024]{0:T(1024)S(1)}, s32[1024]{0:T(1024)}, u32[]{:S(2)}) copy-start(s32[1024]{0:T(1024)} %param.11) | copy-start | bytes 12292
  0.6 0.7 %copy-start.3 = (s32[1024]{0:T(1024)S(1)}, s32[1024]{0:T(1024)}, u32[]{:S(2)}) copy-start(s32[1024]{0:T(1024)} %param.10) | copy-start | bytes 12292
  0.7 0.7 %copy-start.5 = (f32[16]{0:T(128)S(1)}, f32[16]{0:T(128)}, u32[]{:S(2)}) copy-start(f32[16]{0:T(128)} %coef_ref.1) | copy-start | bytes 196
  1.3 1.0 %copy-start = (f32[16,8,8,128]{3,2,1,0:T(8,128)S(1)}, f32[16,8,8,128]{3,2,1,0:T(8,128)}, u32[]{:S(2)}) copy-start(f32[16,8,8,128]{3,2,1,0:T(8,128)} %param.7) | copy-start | bytes 1572868
  2.4 0.8 %copy-start.1 = (f32[8,8,128]{2,1,0:T(8,128)S(1)}, f32[8,8,128]{2,1,0:T(8,128)}, u32[]{:S(2)}) copy-start(f32[8,8,128]{2,1,0:T(8,128)} %param.6) | copy-start | bytes 98308
  3.1 0.8 %copy-start.2 = (s32[8,8,128]{2,1,0:T(8,128)S(1)}, s32[8,8,128]{2,1,0:T(8,128)}, u32[]{:S(2)}) copy-start(s32[8,8,128]{2,1,0:T(8,128)} %param.8) | copy-start | bytes 98308

commit v3 on v2

--- a/solution.py
+++ b/solution.py
@@ -128,10 +128,10 @@
 def kernel(
     n_gx, n_gy,
     e_ref, t_ref, lab_ref, coef_ref, cell_ref, slot_ref,
-    e_out, t_out, rows_out,
-    e_in, lab_in, own, mid, hx0, hx1, pk, hp, own_st, est, tst, wst, sl, bump,
-    a_ref, atk, tab, m_ref, snd, rcv, lhs, rhs,
-    in_sem, out_sem, x_send, x_recv, p_send, p_recv, line_sem, local_sem, all_send, all_recv,
+    mid, rcv,
+    e_in, lab_in, cell_in, slot_in, coef_in, own, hx0, hx1, pk, hp, own_st, est, tst, wst, sl, bump,
+    a_ref, atk, tab, m_ref, snd,
+    in_sem, x_send, x_recv, p_send, p_recv, line_sem, local_sem, all_send, all_recv,
 ):
     n = n_gx * n_gy
     gx, gy = lax.axis_index("gx"), lax.axis_index("gy")
@@ -156,10 +156,22 @@
     def load_t(x):
         return pltpu.make_async_copy(t_ref.at[:, x, :], own.at[x, pl.ds(0, 128), :], in_sem.at[x])
 
+    def load_cell():
+        return pltpu.make_async_copy(cell_ref, cell_in, in_sem.at[10])
+
+    def load_slot():
+        return pltpu.make_async_copy(slot_ref, slot_in, in_sem.at[11])
+
+    def load_coef():
+        return pltpu.make_async_copy(coef_ref, coef_in, in_sem.at[12])
+
     load_e().start()
     load_lab().start()
     for x in range(8):
         load_t(x).start()
+    load_cell().start()
+    load_slot().start()
+    load_coef().start()
     load_e().wait()
     load_lab().wait()
     pair = [[], []]
@@ -213,9 +225,8 @@
         pl.semaphore_signal(line_sem, inc=1, device_id=at(dx, dy), device_id_type=MESH)
     for x in range(8):
         load_t(x).wait()
-    for q in range(4):
-        for d in range(2):
-            send_x(0, q, d).start()
+    for d in range(2):
+        send_x(0, 0, d).start()
 
     def own_rows(ref, item):
         part = pl.ds(pl.multiple_of(item * 8, 8), 8)
@@ -234,11 +245,17 @@
     for group in range(2):
         for dx, dy in corners:
             send_p(0, group, dx, dy).start()
+    for q in range(1, 4):
+        for d in range(2):
+            send_x(0, q, d).start()
 
     tall = lax.broadcasted_iota(jnp.int32, (128, 128), 0).astype(F32)
     wide = lax.broadcasted_iota(jnp.int32, (128, 128), 1).astype(F32)
     eight = lax.broadcasted_iota(jnp.int32, (8, 128), 0).astype(F32)
-    cell, slot = cell_ref[...], slot_ref[...]
+    load_cell().wait()
+    load_slot().wait()
+    load_coef().wait()
+    cell, slot = cell_in[...], slot_in[...]
     owner = (slot // 1024).astype(F32)
     row = slot % 1024
     row_hi, row_lo = (row // 128 + 1).astype(F32), (row % 128).astype(F32)
@@ -341,7 +358,7 @@
             v = scaled - KNOTS[j] * (ROOT / WIDTH)
             b = jnp.exp2(-(v * v))
             bump[(s * COEF + j) * ALL + i] = b
-            cb = coef_ref[j] * b
+            cb = coef_in[j] * b
             total = total + cb
             slope = slope + v * cb
         half = jnp.where(p, 1.0, 0.5)
@@ -440,18 +457,6 @@
 
     lax.fori_loop(0, 4, second_round, 0)
 
-    def store_t(x):
-        return pltpu.make_async_copy(mid.at[x, pl.ds(0, 128), :], t_out.at[:, x, :], out_sem.at[x])
-
-    def store_e():
-        return pltpu.make_async_copy(e_in, e_out, out_sem.at[8])
-
-    for x in range(8):
-        e_in[pl.ds(x, 8, stride=8), :] = mid[x, ENTH * 8 : ENTH * 8 + 8, :]
-    store_e().start()
-    for x in range(8):
-        store_t(x).start()
-
     def top(item):
         v = jnp.broadcast_to(mid[0, item * 8 + 7 : item * 8 + 8, :], (8, 128))
         for x in range(1, 8):
@@ -466,7 +471,7 @@
         v = scaled - KNOTS[j] * (ROOT / WIDTH)
         b = jnp.exp2(-(v * v))
         bumps.append(b)
-        slope = slope + v * (coef_ref[j] * b)
+        slope = slope + v * (coef_in[j] * b)
     slope = jnp.where(p7, 1.0, 0.5) - (2.0 / (WIDTH * ROOT)) * slope
     for f in range(COEF):
         val = slope * top(f) + bumps[f]
@@ -502,6 +507,22 @@
         snd.at[:, rest, :], rcv.at[:, rest, :], all_send, all_recv, device_id=at(1, 0), device_id_type=MESH
     ).wait()
 
+
+def finish(mid, rcv, e_out, t_out, rows_out, e_tile, lhs, rhs, res, sem):
+    def store_t(x):
+        return pltpu.make_async_copy(mid.at[x, pl.ds(0, 128), :], t_out.at[:, x, :], sem.at[x])
+
+    def store_e():
+        return pltpu.make_async_copy(e_tile, e_out, sem.at[8])
+
+    for x in range(8):
+        store_t(x).start()
+    for x in range(8):
+        e_tile[pl.ds(x, 8, stride=8), :] = mid[x, ENTH * 8 : ENTH * 8 + 8, :]
+    store_e().start()
+
+    tall = lax.broadcasted_iota(jnp.int32, (128, 128), 0).astype(F32)
+    eight = lax.broadcasted_iota(jnp.int32, (8, 128), 0).astype(F32)
     where = rcv[4].T
     vals = [rcv[g].T for g in range(4)]
     for k in range(MOST):
@@ -514,7 +535,10 @@
     whole = lhs[...]
     hi = whole.astype(BF16)
     lo = (whole - hi.astype(F32)).astype(BF16)
-    rows_out[...] = nt(hi, rhs[...]) + nt(lo, rhs[...])
+    res[...] = nt(hi, rhs[...]) + nt(lo, rhs[...])
+    for r in range(8):
+        for half in range(2):
+            rows_out[half * 8 : half * 8 + 8, r * 128 : (r + 1) * 128] = res[pl.ds(half * 64 + r, 8, stride=8), :]
     store_e().wait()
     for x in range(8):
         store_t(x).wait()
@@ -523,28 +547,31 @@
 def solution(mesh):
     n_gx, n_gy = mesh.shape["gx"], mesh.shape["gy"]
     vmem = pl.BlockSpec(memory_space=pltpu.VMEM)
-    smem = pl.BlockSpec(memory_space=pltpu.SMEM)
-    hbm = pl.BlockSpec(memory_space=pl.ANY)
+    hbm = pl.BlockSpec(memory_space=pltpu.HBM)
     dma = pltpu.SemaphoreType.DMA
+
+    def in_hbm(x):
+        return pltpu.with_memory_space_constraint(x, pltpu.HBM)
 
     def tiles(*shape):
         return pltpu.VMEM((*shape, 8, 128), F32)
 
     def local(enthalpy_start, tangent_start, labels, curve_parameters, pixel_cells, row_slot):
-        e_end, t_end, rows = pl.pallas_call(
+        mid, rcv = pl.pallas_call(
             functools.partial(kernel, n_gx, n_gy),
             out_shape=[
-                jax.ShapeDtypeStruct((64, 128), F32),
-                jax.ShapeDtypeStruct((128, 8, 128), F32),
-                jax.ShapeDtypeStruct((128, 128), F32),
+                jax.ShapeDtypeStruct((8, 136, 128), F32),
+                jax.ShapeDtypeStruct((5, 128, 128), F32),
             ],
-            in_specs=[hbm, hbm, hbm, smem, vmem, vmem],
-            out_specs=[hbm, hbm, vmem],
+            in_specs=[hbm] * 6,
+            out_specs=[vmem, vmem],
             scratch_shapes=[
                 pltpu.VMEM((64, 128), F32),
                 pltpu.VMEM((64, 128), jnp.int32),
+                pltpu.VMEM((8, 128), jnp.int32),
+                pltpu.VMEM((8, 128), jnp.int32),
+                pltpu.SMEM((COEF,), F32),
                 pltpu.VMEM((8, 144, 128), F32),
-                pltpu.VMEM((8, 136, 128), F32),
                 pltpu.VMEM((2, DEEP, 144, 128), F32),
                 pltpu.VMEM((2, DEEP, 136, 128), F32),
                 pltpu.VMEM((ROUNDS, 2, 40, 128), F32),
@@ -560,27 +587,40 @@
                 pltpu.VMEM((128, 1024), BF16),
                 pltpu.VMEM((1024, 1024), BF16),
                 pltpu.VMEM((5, 128, 128), F32),
-                pltpu.VMEM((5, 128, 128), F32),
-                pltpu.VMEM((128, 4096), F32),
-                pltpu.VMEM((128, 4096), BF16),
-                dma((10,)), dma((9,)),
+                dma((13,)),
                 dma((ROUNDS, 5, 2)), dma((ROUNDS, 5, 2)),
                 dma((ROUNDS, 3, 3, 2)), dma((ROUNDS, 3, 3, 2)),
                 pltpu.SemaphoreType.REGULAR, dma, dma, dma,
             ],
             compiler_params=pltpu.CompilerParams(
-                collective_id=0, has_side_effects=True, vmem_limit_bytes=48 * 2**20
+                collective_id=0, has_side_effects=True, vmem_limit_bytes=40 * 2**20
             ),
             name="steps",
         )(
-            enthalpy_start.reshape(64, 128), tangent_start.reshape(128, 8, 128), labels.reshape(64, 128),
-            curve_parameters, pixel_cells.reshape(8, 128), row_slot.reshape(8, 128),
+            in_hbm(enthalpy_start.reshape(64, 128)), in_hbm(tangent_start.reshape(128, 8, 128)),
+            in_hbm(labels.reshape(64, 128)), in_hbm(curve_parameters),
+            in_hbm(pixel_cells.reshape(8, 128)), in_hbm(row_slot.reshape(8, 128)),
         )
-        return (
-            e_end.reshape(8, 8, 128),
-            t_end.reshape(COEF, 8, 8, 128),
-            rows.reshape(COEF, 1024),
-        )
+        e_end, t_end, rows = pl.pallas_call(
+            finish,
+            out_shape=[
+                jax.ShapeDtypeStruct((64, 128), F32),
+                jax.ShapeDtypeStruct((128, 8, 128), F32),
+                jax.ShapeDtypeStruct((COEF, 1024), F32),
+            ],
+            in_specs=[vmem, vmem],
+            out_specs=[hbm, hbm, vmem],
+            scratch_shapes=[
+                pltpu.VMEM((64, 128), F32),
+                pltpu.VMEM((128, 4096), F32),
+                pltpu.VMEM((128, 4096), BF16),
+                pltpu.VMEM((128, 128), F32),
+                dma((9,)),
+            ],
+            compiler_params=pltpu.CompilerParams(vmem_limit_bytes=40 * 2**20),
+            name="finish",
+        )(mid, rcv)
+        return e_end.reshape(8, 8, 128), t_end.reshape(COEF, 8, 8, 128), rows
 
     in_specs = (
         P(None, "gx", "gy"),

time: 53.5 us -> 44.5 us (0.83)
  local copies, waits for them, and re-layouts: 5.29 us -> 0 us
  Pallas kernels: 47.2 us -> 43.7 us
    pallas_call x1, Pallas kernels: 47.2 us -> 41.5 us  [local(): pl.pallas_call(functools.partial(kernel, n_gx, n_gy), out_shape=[jax.Shap...]
    unnamed x14 -> x0, local copies, waits for them, and re-layouts: 4.64 us -> none
    pallas_call x0 -> x1, Pallas kernels: none -> 2.24 us  [local(): pl.pallas_call(finish, out_shape=[jax.ShapeDtypeStruct((64, 128), F32), j...]
    reshape x1 -> x0, local copies, waits for them, and re-layouts: 0.65 us -> none  [local(): rows.reshape(COEF, 1024)]
where the time goes in v3:
time: 44.5 us; the launch traced here: 44.4 us
  Pallas kernels  43.7 us (98%)
  between operations  0.64 us (1%)
    pallas_call x1, Pallas kernels, local(): pl.pallas_call(functools.partial(kernel, n_gx, n_gy), out_shape=[jax.Shap...  41.5 us
    pallas_call x1, Pallas kernels, local(): pl.pallas_call(finish, out_shape=[jax.ShapeDtypeStruct((64, 128), F32), j...  2.24 us

profile of v3, /device:TPU:1, one launch (start us, length us, event | category | flops | bytes accessed | tf_op | source)
XLA Modules:
  0.0 44.4 jit_solution(3453577902363607374)
XLA Ops:
  0.6 41.5 %steps.1 = (f32[8,136,128]{2,1,0:T(8,128)S(1)}, f32[5,128,128]{2,1,0:T(8,128)S(1)}) custom-call(f32[64,128]{1,0:T(8,128)} %bitcast.8, f32[128,8,128]{2,1,0:T(8,128)} %bitcast.7, s32[64,128]{1,0:T(8,128)} %bitcast.9, f32[16]{0:T(128)} %coef_ref.1, s32[8,128]{1,0:T(8,128)} %bitcast.10, s32[8,128]{1,0:T(8,128)} %bitcast.11), custom_call_target="tpu_custom_call" | custom-call | tf_op jit(solution)/shard_map/steps/pallas_call | solution.py:560
  42.1 2.2 %finish.1 = (f32[64,128]{1,0:T(8,128)}, f32[128,8,128]{2,1,0:T(8,128)}, f32[16,1024]{1,0:T(8,128)}) custom-call(f32[8,136,128]{2,1,0:T(8,128)S(1)} %get-tuple-element.8.mid, f32[5,128,128]{2,1,0:T(8,128)S(1)} %get-tuple-element.9.rcv), custom_call_target="tpu_custom_call" | custom-call | tf_op jit(solution)/shard_map/finish/pallas_call | solution.py:604

commit v4 on v3

--- a/solution.py
+++ b/solution.py
@@ -21,6 +21,7 @@
 ALL = MAIN + STRIP
 ENTH = COEF
 MOST = 32
+GROUPS = ((0, 1, 2, 3),)
 MESH = pl.DeviceIdType.MESH
 F32 = jnp.float32
 BF16 = jnp.bfloat16
@@ -93,28 +94,38 @@
     return out
 
 
-def advance(step, state, temp, wx, wy, wz):
-    new = list(state)
-
-    def own(i, t):
-        fy = wy(i) * (turn(t, -1, 1) - t)
-        fz = wz(i) * (turn(t, -1, 0) - t)
-        return (fy - turn(fy, 1, 1)) + (fz - turn(fz, 1, 0))
-
+def advance(step, fields, load, store, temp, wx, wy, wz):
+    def temps(i):
+        olds = [load(k, i) for k in fields]
+        return olds, [temp(k, i, v) for k, v in zip(fields, olds)]
+
+    def across(i, ts, nexts):
+        w = wx(i)
+        return [w * (b - a) for a, b in zip(ts, nexts)]
+
+    def update(i, olds, ts, fluxes, below):
+        y, z = wy(i), wz(i)
+        for k, old, t, flux, under in zip(fields, olds, ts, fluxes, below):
+            fy = y * (turn(t, -1, 1) - t)
+            fz = z * (turn(t, -1, 0) - t)
+            store(k, i, old + ((flux - under) + ((fy - turn(fy, 1, 1)) + (fz - turn(fz, 1, 0)))))
+
+    both = [temps(i) for i in range(MAIN, ALL)]
+    ts = [t for _, t in both]
+    ts.append([turn(t, -16, 1) for t in ts[0]])
+    fluxes = [across(MAIN + g, ts[g], ts[g + 1]) for g in range(STRIP)]
+    first = [turn(f, 16, 1) for f in fluxes[-1]]
+    for g in range(STRIP):
+        update(MAIN + g, *both[g], fluxes[g], fluxes[g - 1] if g > 0 else first)
     lo, hi = step, MAIN - step
-    t = temp(lo)
-    t_next = temp(lo + 1)
-    flux = wx(lo) * (t_next - t)
+    old, t = temps(lo)
+    old_next, t_next = temps(lo + 1)
+    flux = across(lo, t, t_next)
     for i in range(lo + 1, hi - 1):
-        t, t_next = t_next, temp(i + 1)
-        below, flux = flux, wx(i) * (t_next - t)
-        new[i] = state[i] + ((flux - below) + own(i, t))
-    ts = [temp(i) for i in range(MAIN, ALL)]
-    fluxes = [wx(MAIN + g) * ((ts[g + 1] if g < STRIP - 1 else turn(ts[0], -16, 1)) - ts[g]) for g in range(STRIP)]
-    for g in range(STRIP):
-        below = fluxes[g - 1] if g > 0 else turn(fluxes[-1], 16, 1)
-        new[MAIN + g] = state[MAIN + g] + ((fluxes[g] - below) + own(MAIN + g, ts[g]))
-    return new
+        old, t = old_next, t_next
+        old_next, t_next = temps(i + 1)
+        below, flux = flux, across(i, t, t_next)
+        update(i, old, t, flux, below)
 
 
 def nt(a, b):
@@ -129,7 +140,7 @@
     n_gx, n_gy,
     e_ref, t_ref, lab_ref, coef_ref, cell_ref, slot_ref,
     mid, rcv,
-    e_in, lab_in, cell_in, slot_in, coef_in, own, hx0, hx1, pk, hp, own_st, est, tst, wst, sl, bump,
+    e_in, lab_in, cell_in, slot_in, coef_in, own, hx0, hx1, pk, hp, own_st, est, tst, fst, wst, sl, bump,
     a_ref, atk, tab, m_ref, snd,
     in_sem, x_send, x_recv, p_send, p_recv, line_sem, local_sem, all_send, all_recv,
 ):
@@ -377,6 +388,9 @@
 
         lax.fori_loop(0, (hi - lo) // 4, four, 0)
 
+    def keep_e(k, i, v):
+        est[i] = v
+
     def enthalpy(r):
         start = all_rows(r, ENTH, 4, 0)
         for i in range(ALL):
@@ -384,11 +398,7 @@
         for s in range(DEEP):
             shape_rows(s, s, MAIN - s)
             shape_rows(s, MAIN, ALL)
-            state = [est[i] for i in range(ALL)]
-            new = advance(s, state, lambda i: tst[i], *weights)
-            for i in range(ALL):
-                if new[i] is not state[i]:
-                    est[i] = new[i]
+            advance(s, [0], lambda k, i: est[i], keep_e, lambda k, i, v: tst[i], *weights)
         state = [est[i] for i in range(ALL)]
         done = merge(state)
         for x in range(8):
@@ -398,23 +408,30 @@
             last, first = pack_edges(state[MAIN:], 0, None, None)
             store_pack(1, 4, last, first)
 
+    def keep_t(k, i, v):
+        fst[k * ALL + i] = v
+
     def tangents(r, q):
         last = first = None
-        for it in range(4):
-            j = q * 4 + it
-            state = all_rows(r, j, q, it)
+        for its in GROUPS:
+            for it in its:
+                for i, v in enumerate(all_rows(r, q * 4 + it, q, it)):
+                    fst[it * ALL + i] = v
             for s in range(DEEP):
-                def temp(i, s=s, state=state):
-                    return sl[s * ALL + i] * state[i] + bump[(s * COEF + j) * ALL + i]
-
-                state = advance(s, state, temp, *weights)
-            done = merge(state)
-            part = pl.ds(pl.multiple_of(j * 8, 8), 8)
-            for x in range(8):
-                mid[x, part, :] = done[x]
-            if r == 0:
-                store_strips(j, state[MAIN:])
-                last, first = pack_edges(state[MAIN:], it, last, first)
+                def temp(k, i, v, s=s):
+                    return sl[s * ALL + i] * v + bump[(s * COEF + q * 4 + k) * ALL + i]
+
+                advance(s, its, lambda k, i: fst[k * ALL + i], keep_t, temp, *weights)
+            for it in its:
+                j = q * 4 + it
+                state = [fst[it * ALL + i] for i in range(ALL)]
+                done = merge(state)
+                part = pl.ds(pl.multiple_of(j * 8, 8), 8)
+                for x in range(8):
+                    mid[x, part, :] = done[x]
+                if r == 0:
+                    store_strips(j, state[MAIN:])
+                    last, first = pack_edges(state[MAIN:], it, last, first)
         if r == 0:
             store_pack(1, q, last, first)
 
@@ -579,6 +596,7 @@
                 tiles((COEF + 2) * STRIP),
                 tiles(2 * ALL),
                 tiles(ALL),
+                tiles(4 * ALL),
                 tiles(3 * ALL),
                 tiles(DEEP * ALL),
                 tiles(DEEP * COEF * ALL),

time: 44.5 us -> 43.2 us (0.971)
  Pallas kernels: 43.7 us -> 42.4 us
    pallas_call x1, Pallas kernels: 41.5 us -> 40.2 us  [local(): pl.pallas_call(functools.partial(kernel, n_gx, n_gy), out_shape=[jax.Shap...]
where the time goes in v4:
time: 43.2 us; the launch traced here: 43.1 us
  Pallas kernels  42.4 us (98%)
  between operations  0.64 us (1%)
    pallas_call x1, Pallas kernels, local(): pl.pallas_call(functools.partial(kernel, n_gx, n_gy), out_shape=[jax.Shap...  40.2 us
    pallas_call x1, Pallas kernels, local(): pl.pallas_call(finish, out_shape=[jax.ShapeDtypeStruct((64, 128), F32), j...  2.24 us

profile of v4, /device:TPU:1, one launch (start us, length us, event | category | flops | bytes accessed | tf_op | source)
XLA Modules:
  0.0 43.1 jit_solution(14127800120379678926)
XLA Ops:
  0.6 40.2 %steps.1 = (f32[8,136,128]{2,1,0:T(8,128)S(1)}, f32[5,128,128]{2,1,0:T(8,128)S(1)}) custom-call(f32[64,128]{1,0:T(8,128)} %bitcast.8, f32[128,8,128]{2,1,0:T(8,128)} %bitcast.7, s32[64,128]{1,0:T(8,128)} %bitcast.9, f32[16]{0:T(128)} %coef_ref.1, s32[8,128]{1,0:T(8,128)} %bitcast.10, s32[8,128]{1,0:T(8,128)} %bitcast.11), custom_call_target="tpu_custom_call" | custom-call | tf_op jit(solution)/shard_map/steps/pallas_call | solution.py:577
  40.8 2.2 %finish.1 = (f32[64,128]{1,0:T(8,128)}, f32[128,8,128]{2,1,0:T(8,128)}, f32[16,1024]{1,0:T(8,128)}) custom-call(f32[8,136,128]{2,1,0:T(8,128)S(1)} %get-tuple-element.8.mid, f32[5,128,128]{2,1,0:T(8,128)S(1)} %get-tuple-element.9.rcv), custom_call_target="tpu_custom_call" | custom-call | tf_op jit(solution)/shard_map/finish/pallas_call | solution.py:622

commit v5 on v4

--- a/solution.py
+++ b/solution.py
@@ -62,6 +62,21 @@
     return last, first
 
 
+def widen(edges):
+    lane = lanes()
+    low, own, high = edges
+    out = []
+    for h in range(2):
+        v = None
+        for g in (2 * h, 2 * h + 1):
+            base = 64 * (g % 2)
+            v = place(v, (lane >= base + 16) & (lane < base + 48), turn(own, base + 16 - 32 * g, 1))
+            v = place(v, lane // 16 == base // 16, turn(low, base - 16 - 32 * g, 1))
+            v = place(v, lane // 16 == base // 16 + 3, turn(high, base + 48 - 32 * g, 1))
+        out.append(v)
+    return out
+
+
 def full_strips(own, low, high, before, after, it):
     lane = lanes()
     block, inside = lane // 16, lane % 16
@@ -72,14 +87,9 @@
         v = place(v, block == 3, turn(high[g], 52, 1))
         v = place(v, block == 4, turn(low[g], -52, 1))
         v = place(v, block == 7, turn(high[g], -4, 1))
-        at = 32 * g + 4 * it
-        first, last = inside < 4, inside >= 12
-        v = place(v, ((block == 1) | (block == 2)) & first, turn(before[1], 16 - at, 1))
-        v = place(v, (block == 0) & first, turn(before[0], -16 - at, 1))
-        v = place(v, (block == 3) & first, turn(before[2], 48 - at, 1))
-        v = place(v, ((block == 5) | (block == 6)) & last, turn(after[1], 92 - at, 1))
-        v = place(v, (block == 4) & last, turn(after[0], 60 - at, 1))
-        v = place(v, (block == 7) & last, turn(after[2], 124 - at, 1))
+        at = 64 * (g % 2) + 4 * it
+        v = place(v, (block < 4) & (inside < 4), turn(before[g // 2], -at, 1))
+        v = place(v, (block >= 4) & (inside >= 12), turn(after[g // 2], 76 - at, 1))
         out.append(v)
     return out
 
@@ -141,8 +151,8 @@
     e_ref, t_ref, lab_ref, coef_ref, cell_ref, slot_ref,
     mid, rcv,
     e_in, lab_in, cell_in, slot_in, coef_in, own, hx0, hx1, pk, hp, own_st, est, tst, fst, wst, sl, bump,
-    a_ref, atk, tab, m_ref, snd,
-    in_sem, x_send, x_recv, p_send, p_recv, line_sem, local_sem, all_send, all_recv,
+    a_ref, atk, tab, m_ref, top_st, snd,
+    in_sem, x_send, x_recv, p_send, p_recv, near_sem, local_sem, all_send, all_recv,
 ):
     n = n_gx * n_gy
     gx, gy = lax.axis_index("gx"), lax.axis_index("gy")
@@ -152,10 +162,18 @@
         return lax.rem(gx + dx + n_gx, n_gx), lax.rem(gy + dy + n_gy, n_gy)
 
     corners = [(dx, dy) for dx in (0, -1, 1) for dy in (-1, 1)]
-    line = [(dx, 0) for dx in range(1, n_gx)]
-    greeted = line + [(0, dy) for dy in range(1, n_gy)] + [c for c in corners if c[0] != 0]
+    around = corners + [(-1, 0), (1, 0)]
+    rounds = [around, [(2 * dx, 2 * dy) for dx, dy in around], [(-4, 0), (4, 0)]]
+
+    def greet(k):
+        for dx, dy in rounds[k]:
+            pl.semaphore_signal(near_sem.at[k], inc=1, device_id=at(dx, dy), device_id_type=MESH)
+
+    def greeted(k):
+        pl.semaphore_wait(near_sem.at[k], len(rounds[k]))
+
     barrier = pltpu.get_barrier_semaphore()
-    for dx, dy in greeted:
+    for dx, dy in around:
         pl.semaphore_signal(barrier, inc=1, device_id=at(dx, dy), device_id_type=MESH)
 
     def load_e():
@@ -227,13 +245,11 @@
         last, first = pack_edges(strips, k, last, first)
     store_pack(0, 4, last, first)
 
-    pl.semaphore_wait(barrier, len(greeted))
+    pl.semaphore_wait(barrier, len(around))
     for d in range(2):
         send_x(0, 4, d).start()
     for dx, dy in corners:
         send_p(0, 2, dx, dy).start()
-    for dx, dy in line:
-        pl.semaphore_signal(line_sem, inc=1, device_id=at(dx, dy), device_id_type=MESH)
     for x in range(8):
         load_t(x).wait()
     for d in range(2):
@@ -259,6 +275,8 @@
     for q in range(1, 4):
         for d in range(2):
             send_x(0, q, d).start()
+
+    greet(0)
 
     tall = lax.broadcasted_iota(jnp.int32, (128, 128), 0).astype(F32)
     wide = lax.broadcasted_iota(jnp.int32, (128, 128), 1).astype(F32)
@@ -297,18 +315,48 @@
         tab[2 * MOST : 4 * MOST, cols] = jnp.zeros((2 * MOST, 128), BF16)
     snd[4] = nt(a_ref[...], tab[...])
 
+    def shape_row(r, s, i):
+        e = est[i]
+        p = est[ALL + i] > 0
+        scaled = jnp.where(p, e, 100.0) * (ROOT / WIDTH)
+        total = jnp.zeros((8, 128), F32)
+        slope = jnp.zeros((8, 128), F32)
+        for j in range(COEF):
+            v = scaled - KNOTS[j] * (ROOT / WIDTH)
+            b = jnp.exp2(-(v * v))
+            bump[((r * DEEP + s) * COEF + j) * ALL + i] = b
+            cb = coef_in[j] * b
+            total = total + cb
+            slope = slope + v * cb
+        half = jnp.where(p, 1.0, 0.5)
+        tst[i] = half * e + total
+        sl[(r * DEEP + s) * ALL + i] = half - (2.0 / (WIDTH * ROOT)) * slope
+
+    def shape_rows(r, s, lo, hi):
+        for i in range(lo, lo + (hi - lo) % 4):
+            shape_row(r, s, i)
+        lo += (hi - lo) % 4
+
+        def four(k, _):
+            for i in range(4):
+                shape_row(r, s, lo + k * 4 + i)
+            return 0
+
+        lax.fori_loop(0, (hi - lo) // 4, four, 0)
+
     def halo_rows(r, d, item):
         part = pl.ds(pl.multiple_of(item * 8, 8), 8)
         return [halos[r][d, x, part, :] for x in range(DEEP)]
 
-    def all_rows(r, item, q, it):
+    def wide_edges(r, q):
+        part = pl.ds(pl.multiple_of(q * 8, 8), 8)
+        return [widen([hp[r, k, side, part, :] for k in range(3)]) for side in range(2)]
+
+    def all_rows(r, item, wide, it):
         low, high = halo_rows(r, 0, item), halo_rows(r, 1, item)
         main = low + own_rows(own if r == 0 else mid, item) + high
-        part = pl.ds(pl.multiple_of(q * 8, 8), 8)
-        before = [hp[r, k, 0, part, :] for k in range(3)]
-        after = [hp[r, k, 1, part, :] for k in range(3)]
         strips = [own_st[item * STRIP + g] for g in range(STRIP)]
-        return main + full_strips(strips, low, high, before, after, it)
+        return main + full_strips(strips, low, high, *wide, it)
 
     def wait_e(r):
         for d in range(2):
@@ -316,8 +364,12 @@
         for dx, dy in corners:
             send_p(r, 2, dx, dy).wait()
 
+    for x in range(8):
+        est[DEEP + x] = own[x, ENTH * 8 : ENTH * 8 + 8, :]
+        est[ALL + DEEP + x] = own[x, (ENTH + 1) * 8 : (ENTH + 2) * 8, :]
+    shape_rows(0, 0, DEEP, MAIN - DEEP)
     wait_e(0)
-    pcm = all_rows(0, ENTH + 1, 4, 1)
+    pcm = all_rows(0, ENTH + 1, wide_edges(0, 4), 1)
     for i in range(ALL):
         est[ALL + i] = pcm[i]
 
@@ -359,45 +411,20 @@
 
     weights = (lambda i: wst[i], lambda i: wst[ALL + i], lambda i: wst[2 * ALL + i])
 
-    def shape_row(s, i):
-        e = est[i]
-        p = est[ALL + i] > 0
-        scaled = jnp.where(p, e, 100.0) * (ROOT / WIDTH)
-        total = jnp.zeros((8, 128), F32)
-        slope = jnp.zeros((8, 128), F32)
-        for j in range(COEF):
-            v = scaled - KNOTS[j] * (ROOT / WIDTH)
-            b = jnp.exp2(-(v * v))
-            bump[(s * COEF + j) * ALL + i] = b
-            cb = coef_in[j] * b
-            total = total + cb
-            slope = slope + v * cb
-        half = jnp.where(p, 1.0, 0.5)
-        tst[i] = half * e + total
-        sl[s * ALL + i] = half - (2.0 / (WIDTH * ROOT)) * slope
-
-    def shape_rows(s, lo, hi):
-        for i in range(lo, lo + (hi - lo) % 4):
-            shape_row(s, i)
-        lo += (hi - lo) % 4
-
-        def four(k, _):
-            for i in range(4):
-                shape_row(s, lo + k * 4 + i)
-            return 0
-
-        lax.fori_loop(0, (hi - lo) // 4, four, 0)
-
     def keep_e(k, i, v):
         est[i] = v
 
     def enthalpy(r):
-        start = all_rows(r, ENTH, 4, 0)
+        start = all_rows(r, ENTH, wide_edges(r, 4), 0)
         for i in range(ALL):
             est[i] = start[i]
         for s in range(DEEP):
-            shape_rows(s, s, MAIN - s)
-            shape_rows(s, MAIN, ALL)
+            if r == 0 and s == 0:
+                shape_rows(r, s, 0, DEEP)
+                shape_rows(r, s, MAIN - DEEP, ALL)
+            else:
+                shape_rows(r, s, s, MAIN - s)
+                shape_rows(r, s, MAIN, ALL)
             advance(s, [0], lambda k, i: est[i], keep_e, lambda k, i, v: tst[i], *weights)
         state = [est[i] for i in range(ALL)]
         done = merge(state)
@@ -413,13 +440,14 @@
 
     def tangents(r, q):
         last = first = None
+        wide = wide_edges(r, q)
         for its in GROUPS:
             for it in its:
-                for i, v in enumerate(all_rows(r, q * 4 + it, q, it)):
+                for i, v in enumerate(all_rows(r, q * 4 + it, wide, it)):
                     fst[it * ALL + i] = v
             for s in range(DEEP):
                 def temp(k, i, v, s=s):
-                    return sl[s * ALL + i] * v + bump[(s * COEF + q * 4 + k) * ALL + i]
+                    return sl[(r * DEEP + s) * ALL + i] * v + bump[((r * DEEP + s) * COEF + q * 4 + k) * ALL + i]
 
                 advance(s, its, lambda k, i: fst[k * ALL + i], keep_t, temp, *weights)
             for it in its:
@@ -436,6 +464,8 @@
             store_pack(1, q, last, first)
 
     enthalpy(0)
+    greeted(0)
+    greet(1)
     for d in range(2):
         send_x(1, 4, d).start()
     for dx, dy in corners:
@@ -448,18 +478,50 @@
         for d in range(2):
             send_x(0, q, d).wait()
         tangents(0, q)
-        for d in range(2):
-            send_x(1, q, d).start()
         for group in range(2):
             @pl.when(q == 2 * group + 1)
             def _():
                 for dx, dy in corners:
                     send_p(1, group, dx, dy).start()
+        for d in range(2):
+            send_x(1, q, d).start()
         return 0
 
     lax.fori_loop(0, 4, first_round, 0)
+    greeted(1)
+    greet(2)
     wait_e(1)
     enthalpy(1)
+
+    def top(item):
+        v = jnp.broadcast_to(mid[0, pl.ds(item * 8 + 7, 1), :], (8, 128))
+        for x in range(1, 8):
+            v = jnp.where(eight == x, mid[x, pl.ds(item * 8 + 7, 1), :], v)
+        return v
+
+    p7 = jnp.where(lab_in[56:64, :] == 1, 1.0, 0.0) > 0
+    scaled = jnp.where(p7, top(ENTH), 100.0) * (ROOT / WIDTH)
+    slope = jnp.zeros((8, 128), F32)
+    for j in range(COEF):
+        v = scaled - KNOTS[j] * (ROOT / WIDTH)
+        b = jnp.exp2(-(v * v))
+        top_st[j] = b
+        slope = slope + v * (coef_in[j] * b)
+    top_st[COEF] = jnp.where(p7, 1.0, 0.5) - (2.0 / (WIDTH * ROOT)) * slope
+
+    def pack_rows(q):
+        for it in range(4):
+            f = q * 4 + it
+            val = top_st[COEF] * top(f) + top_st[f]
+            hi = val.astype(BF16).astype(F32)
+            lo = val - hi
+            for x in range(8):
+                cols = slice(x * 128, (x + 1) * 128)
+                at_k = atk[x]
+                m_ref[it * MOST : (it + 1) * MOST, cols] = (at_k * hi[x : x + 1]).astype(BF16)
+                m_ref[128 + it * MOST : 128 + (it + 1) * MOST, cols] = (at_k * lo[x : x + 1]).astype(BF16)
+        both = nt(a_ref[...], m_ref[...])
+        snd[q] = both[:, :128] + both[:, 128:]
 
     def second_round(q, _):
         for group in range(2):
@@ -470,41 +532,12 @@
         for d in range(2):
             send_x(1, q, d).wait()
         tangents(1, q)
+        pack_rows(q)
         return 0
 
     lax.fori_loop(0, 4, second_round, 0)
 
-    def top(item):
-        v = jnp.broadcast_to(mid[0, item * 8 + 7 : item * 8 + 8, :], (8, 128))
-        for x in range(1, 8):
-            v = jnp.where(eight == x, mid[x, item * 8 + 7 : item * 8 + 8, :], v)
-        return v
-
-    p7 = jnp.where(lab_in[56:64, :] == 1, 1.0, 0.0) > 0
-    scaled = jnp.where(p7, top(ENTH), 100.0) * (ROOT / WIDTH)
-    slope = jnp.zeros((8, 128), F32)
-    bumps = []
-    for j in range(COEF):
-        v = scaled - KNOTS[j] * (ROOT / WIDTH)
-        b = jnp.exp2(-(v * v))
-        bumps.append(b)
-        slope = slope + v * (coef_in[j] * b)
-    slope = jnp.where(p7, 1.0, 0.5) - (2.0 / (WIDTH * ROOT)) * slope
-    for f in range(COEF):
-        val = slope * top(f) + bumps[f]
-        hi = val.astype(BF16).astype(F32)
-        lo = val - hi
-        for x in range(8):
-            cols = slice(x * 128, (x + 1) * 128)
-            at_k = atk[x]
-            m_ref[f * MOST : (f + 1) * MOST, cols] = (at_k * hi[x : x + 1]).astype(BF16)
-            m_ref[(COEF + f) * MOST : (COEF + f + 1) * MOST, cols] = (at_k * lo[x : x + 1]).astype(BF16)
-    for g in range(4):
-        hi = nt(a_ref[...], m_ref[g * 128 : (g + 1) * 128, :])
-        lo = nt(a_ref[...], m_ref[512 + g * 128 : 512 + (g + 1) * 128, :])
-        snd[g] = hi + lo
-
-    pl.semaphore_wait(line_sem, len(line))
+    greeted(2)
     mine = pl.ds(me, 1)
     keep = pltpu.make_async_copy(snd.at[:, mine, :], rcv.at[:, mine, :], local_sem)
     keep.start()
@@ -552,7 +585,8 @@
     whole = lhs[...]
     hi = whole.astype(BF16)
     lo = (whole - hi.astype(F32)).astype(BF16)
-    res[...] = nt(hi, rhs[...]) + nt(lo, rhs[...])
+    both = nt(jnp.concatenate([hi, lo], 0), rhs[...])
+    res[...] = both[:128] + both[128:]
     for r in range(8):
         for half in range(2):
             rows_out[half * 8 : half * 8 + 8, r * 128 : (r + 1) * 128] = res[pl.ds(half * 64 + r, 8, stride=8), :]
@@ -598,17 +632,18 @@
                 tiles(ALL),
                 tiles(4 * ALL),
                 tiles(3 * ALL),
-                tiles(DEEP * ALL),
-                tiles(DEEP * COEF * ALL),
+                tiles(ROUNDS * DEEP * ALL),
+                tiles(ROUNDS * DEEP * COEF * ALL),
                 pltpu.VMEM((128, 1024), BF16),
                 pltpu.VMEM((8, MOST, 128), F32),
                 pltpu.VMEM((128, 1024), BF16),
-                pltpu.VMEM((1024, 1024), BF16),
+                pltpu.VMEM((256, 1024), BF16),
+                tiles(COEF + 1),
                 pltpu.VMEM((5, 128, 128), F32),
                 dma((13,)),
                 dma((ROUNDS, 5, 2)), dma((ROUNDS, 5, 2)),
                 dma((ROUNDS, 3, 3, 2)), dma((ROUNDS, 3, 3, 2)),
-                pltpu.SemaphoreType.REGULAR, dma, dma, dma,
+                pltpu.SemaphoreType.REGULAR((3,)), dma, dma, dma,
             ],
             compiler_params=pltpu.CompilerParams(
                 collective_id=0, has_side_effects=True, vmem_limit_bytes=40 * 2**20

time: 43.2 us -> 41.2 us (0.954)
  Pallas kernels: 42.4 us -> 40.5 us
    pallas_call x1, Pallas kernels: 40.2 us -> 38.2 us  [local(): pl.pallas_call(functools.partial(kernel, n_gx, n_gy), out_shape=[jax.Shap...]
where the time goes in v5:
time: 41.2 us; the launch traced here: 41.1 us
  Pallas kernels  40.5 us (98%)
  between operations  0.64 us (2%)
    pallas_call x1, Pallas kernels, local(): pl.pallas_call(functools.partial(kernel, n_gx, n_gy), out_shape=[jax.Shap...  38.2 us
    pallas_call x1, Pallas kernels, local(): pl.pallas_call(finish, out_shape=[jax.ShapeDtypeStruct((64, 128), F32), j...  2.22 us

profile of v5, /device:TPU:1, one launch (start us, length us, event | category | flops | bytes accessed | tf_op | source)
XLA Modules:
  0.0 41.1 jit_solution(712696556396186095)
XLA Ops:
  0.6 38.2 %steps.1 = (f32[8,136,128]{2,1,0:T(8,128)S(1)}, f32[5,128,128]{2,1,0:T(8,128)S(1)}) custom-call(f32[64,128]{1,0:T(8,128)} %bitcast.8, f32[128,8,128]{2,1,0:T(8,128)} %bitcast.7, s32[64,128]{1,0:T(8,128)} %bitcast.9, f32[16]{0:T(128)} %coef_ref.1, s32[8,128]{1,0:T(8,128)} %bitcast.10, s32[8,128]{1,0:T(8,128)} %bitcast.11), custom_call_target="tpu_custom_call" | custom-call | tf_op jit(solution)/shard_map/steps/pallas_call | solution.py:611
  38.9 2.2 %finish.1 = (f32[64,128]{1,0:T(8,128)}, f32[128,8,128]{2,1,0:T(8,128)}, f32[16,1024]{1,0:T(8,128)}) custom-call(f32[8,136,128]{2,1,0:T(8,128)S(1)} %get-tuple-element.8.mid, f32[5,128,128]{2,1,0:T(8,128)S(1)} %get-tuple-element.9.rcv), custom_call_target="tpu_custom_call" | custom-call | tf_op jit(solution)/shard_map/finish/pallas_call | solution.py:657

commit v6 on v5

--- a/solution.py
+++ b/solution.py
@@ -161,7 +161,7 @@
     def at(dx, dy):
         return lax.rem(gx + dx + n_gx, n_gx), lax.rem(gy + dy + n_gy, n_gy)
 
-    corners = [(dx, dy) for dx in (0, -1, 1) for dy in (-1, 1)]
+    corners = [(dx, dy) for dx in (-1, 1, 0) for dy in (-1, 1)]
     around = corners + [(-1, 0), (1, 0)]
     rounds = [around, [(2 * dx, 2 * dy) for dx, dy in around], [(-4, 0), (4, 0)]]
 
@@ -221,7 +221,7 @@
         )
 
     def send_p(r, group, dx, dy):
-        part = pl.ds(group * 16, 16) if group < 2 else pl.ds(32, 8)
+        part = pl.ds(32, 8) if group == 2 else pl.ds(0, 32) if r == 0 else pl.ds(group * 16, 16)
         side = 0 if dy == 1 else 1
         return pltpu.make_async_remote_copy(
             pk.at[r, side, part], hp.at[r, 1 - dx, side, part],
@@ -246,10 +246,10 @@
     store_pack(0, 4, last, first)
 
     pl.semaphore_wait(barrier, len(around))
+    for dx, dy in corners:
+        send_p(0, 2, dx, dy).start()
     for d in range(2):
         send_x(0, 4, d).start()
-    for dx, dy in corners:
-        send_p(0, 2, dx, dy).start()
     for x in range(8):
         load_t(x).wait()
     for d in range(2):
@@ -269,9 +269,8 @@
         return 0
 
     lax.fori_loop(0, 4, pack_quad, 0)
-    for group in range(2):
-        for dx, dy in corners:
-            send_p(0, group, dx, dy).start()
+    for dx, dy in corners:
+        send_p(0, 0, dx, dy).start()
     for q in range(1, 4):
         for d in range(2):
             send_x(0, q, d).start()
@@ -333,16 +332,8 @@
         sl[(r * DEEP + s) * ALL + i] = half - (2.0 / (WIDTH * ROOT)) * slope
 
     def shape_rows(r, s, lo, hi):
-        for i in range(lo, lo + (hi - lo) % 4):
+        for i in range(lo, hi):
             shape_row(r, s, i)
-        lo += (hi - lo) % 4
-
-        def four(k, _):
-            for i in range(4):
-                shape_row(r, s, lo + k * 4 + i)
-            return 0
-
-        lax.fori_loop(0, (hi - lo) // 4, four, 0)
 
     def halo_rows(r, d, item):
         part = pl.ds(pl.multiple_of(item * 8, 8), 8)
@@ -466,13 +457,12 @@
     enthalpy(0)
     greeted(0)
     greet(1)
+    for dx, dy in corners:
+        send_p(1, 2, dx, dy).start()
     for d in range(2):
         send_x(1, 4, d).start()
     for dx, dy in corners:
-        send_p(1, 2, dx, dy).start()
-    for group in range(2):
-        for dx, dy in corners:
-            send_p(0, group, dx, dy).wait()
+        send_p(0, 0, dx, dy).wait()
 
     def first_round(q, _):
         for d in range(2):

time: 41.2 us -> 40.9 us (level)
  no operation moved by 1% of the time
where the time goes in v6:
time: 40.9 us; the launch traced here: 40.8 us
  Pallas kernels  40.1 us (98%)
  between operations  0.64 us (2%)
    pallas_call x1, Pallas kernels, local(): pl.pallas_call(functools.partial(kernel, n_gx, n_gy), out_shape=[jax.Shap...  37.9 us
    pallas_call x1, Pallas kernels, local(): pl.pallas_call(finish, out_shape=[jax.ShapeDtypeStruct((64, 128), F32), j...  2.22 us

profile of v6, /device:TPU:1, one launch (start us, length us, event | category | flops | bytes accessed | tf_op | source)
XLA Modules:
  0.0 40.8 jit_solution(4788573479745609483)
XLA Ops:
  0.6 37.9 %steps.1 = (f32[8,136,128]{2,1,0:T(8,128)S(1)}, f32[5,128,128]{2,1,0:T(8,128)S(1)}) custom-call(f32[64,128]{1,0:T(8,128)} %bitcast.8, f32[128,8,128]{2,1,0:T(8,128)} %bitcast.7, s32[64,128]{1,0:T(8,128)} %bitcast.9, f32[16]{0:T(128)} %coef_ref.1, s32[8,128]{1,0:T(8,128)} %bitcast.10, s32[8,128]{1,0:T(8,128)} %bitcast.11), custom_call_target="tpu_custom_call" | custom-call | tf_op jit(solution)/shard_map/steps/pallas_call | solution.py:601
  38.6 2.2 %finish.1 = (f32[64,128]{1,0:T(8,128)}, f32[128,8,128]{2,1,0:T(8,128)}, f32[16,1024]{1,0:T(8,128)}) custom-call(f32[8,136,128]{2,1,0:T(8,128)S(1)} %get-tuple-element.8.mid, f32[5,128,128]{2,1,0:T(8,128)S(1)} %get-tuple-element.9.rcv), custom_call_target="tpu_custom_call" | custom-call | tf_op jit(solution)/shard_map/finish/pallas_call | solution.py:647
